TPU v7x, 512 devices: a whole 4x4x16 slice. The times are simulated.
512 devices in a mesh: gx: 8 (over y, core), gy: 4 (over x), gz: 16 (over z).
Axes of the slice: x: 4, y: 4, z: 16, core: 2. Of those that a mesh axis runs over, the one named last changes fastest.
Arguments:
- right_side: float32 [40, 8, 4, 8192], P(None, 'gx', 'gy', 'gz'), may hold values from -16 to 16
- elem_faces: int32 [4, 8, 4, 4096], P(None, 'gx', 'gy', 'gz'), may hold values from 0 to 895
- elem_class: int32 [8, 4, 4096], P('gx', 'gy', 'gz'), may hold values from 0 to 1
- elem_scale: float32 [8, 4, 4096], P('gx', 'gy', 'gz'), may hold values from 0.5 to 2
- stretch: float32 [3, 8, 4, 4096], P(None, 'gx', 'gy', 'gz'), may hold values from 0.25 to 4
- pml_flag: int32 [8, 4, 4096], P('gx', 'gy', 'gz'), may hold values from 0 to 1, as said below
- send_faces: int32 [6, 8, 4, 1024], P(None, 'gx', 'gy', 'gz'), may hold values from 0 to 511, as said below
- blocks: float32 [2, 3, 2, 6400], replicated, may hold values from -0.5 to 0.5
Outputs:
- solution_field: float32 [40, 8, 4, 8192], P(None, 'gx', 'gy', 'gz')
- residual: float32 [40, 8, 4, 8192], P(None, 'gx', 'gy', 'gz')
Inputs may be any that keep to these rules, and one draw needn't show every extreme that they name: `pml_flag`: on a device at position k along gz, with n devices along gz, h = n // 2 and t = min(k, n - 1 - k), exactly 64 * (h - 1 - t) // (h - 1) elements are flagged; devices at positions k and k + h together hold at most 64. `send_faces`: the 384 entries of one device are different faces.
All inputs are finite; a program needn't handle non-finite values.
Results may differ from a plain program's by a relative error of at most 0.0003.
Values sent between devices are 32-bit elements; how exact they have to be, the bound alone decides.
A program may use at most 128 MiB of HBM per device.

v0:
```python
import jax
import jax.numpy as jnp
from jax import lax
from jax.sharding import PartitionSpec as P

DOF = 20
ITERS = 4
PML_MAX = 64


SIGMA = 1.0
HIGHEST = lax.Precision.HIGHEST


def with_halo(value, sides, width):
    for axis, dim in sides:
        devices, length = (lax.axis_size(axis), value.shape[dim])
        up = [(i, (i + 1) % devices) for i in range(devices - 1)]
        down = [(j, i) for i, j in up]
        last = lax.slice_in_dim(value, length - width, length, axis=dim)
        first = lax.slice_in_dim(value, 0, width, axis=dim)
        before = lax.ppermute(last, axis, up)
        after = lax.ppermute(first, axis, down)
        value = jnp.concatenate([before, value, after], axis=dim)
    return value


def real_split(blocks):
    classes = blocks.shape[0]
    unknowns = DOF
    real_part = blocks[:, :, 0].reshape(classes, 3, 4, unknowns, 4, unknowns)
    imag_part = blocks[:, :, 1].reshape(classes, 3, 4, unknowns, 4, unknowns)
    upper_row = jnp.stack([real_part, -imag_part], axis=5)
    lower_row = jnp.stack([imag_part, real_part], axis=5)
    joined = jnp.stack([upper_row, lower_row], axis=3)
    joined = joined.transpose(0, 1, 3, 4, 2, 6, 7, 5)
    return joined.reshape(classes * 3, 8 * unknowns, 8 * unknowns)


def trade_faces(stacked):
    along_gx = with_halo(stacked[:, 0:2], (("gx", 1),), 1)
    along_gy = with_halo(stacked[:, 2:4], (("gy", 1),), 1)
    along_gz = with_halo(stacked[:, 4:6], (("gz", 1),), 1)
    return jnp.concatenate(
        [
            along_gx[:, 0:1],
            along_gx[:, 3:4],
            along_gy[:, 0:1],
            along_gy[:, 3:4],
            along_gz[:, 0:1],
            along_gz[:, 3:4],
        ],
        axis=1,
    )


def residual_sum(residual):
    return lax.psum(jnp.sum(residual * residual), ("gx", "gy", "gz"))


def local(right_side, elem_faces, elem_class, elem_scale, stretch, pml_flag, send_faces, blocks):
    trace_width = right_side.shape[0]
    source = right_side.reshape(trace_width, -1)
    face_count = source.shape[1]
    elem_map = elem_faces.reshape(4, -1)
    elements = elem_map.shape[1]
    border_faces = send_faces.reshape(6, -1)
    border = border_faces.shape[1]
    classes = blocks.shape[0]
    member_class = elem_class.reshape(-1)
    scaling = elem_scale.reshape(-1)
    stretch_rows = stretch.reshape(3, -1)
    marked = pml_flag.reshape(-1)
    real_blocks = real_split(blocks)
    split_four = real_blocks.reshape(classes, 3, real_blocks.shape[1], real_blocks.shape[2])
    gram_blocks = jnp.einsum("rdji,rdjk->rik", split_four, split_four, precision=HIGHEST)
    onehot = (member_class[None, :] == jnp.arange(classes, dtype=jnp.int32)[:, None]).astype(
        jnp.float32
    )
    base_coef = onehot * scaling[None, :]
    stretch_coef = (onehot[:, None, :] * (scaling[None, :] * (stretch_rows - 1.0))[None]).reshape(
        classes * 3, elements
    )
    capacity = PML_MAX
    running = jnp.cumsum(marked, dtype=jnp.int32)
    position = running - 1
    position = jnp.where(marked > 0, position, capacity)
    pml_rows = (
        jnp.zeros((capacity,), jnp.int32)
        .at[position]
        .set(jnp.arange(elements, dtype=jnp.int32), mode="drop")
    )
    occupied = jnp.zeros((capacity,), jnp.float32).at[position].set(1.0, mode="drop")
    pml_weight = stretch_coef[:, pml_rows] * occupied[None, :]
    solution = jnp.zeros_like(source)
    residual = source
    direction = source
    norm_now = residual_sum(residual)
    for iteration in range(ITERS):
        outgoing = direction[:, border_faces]
        incoming = trade_faces(outgoing)
        extended = jnp.concatenate([direction, incoming.reshape(trace_width, 6 * border)], axis=1)
        gathered = extended[:, elem_map].reshape(4 * trace_width, elements)
        products = jnp.einsum("rij,je->rie", gram_blocks, gathered, precision=HIGHEST)
        result = jnp.sum(products * base_coef[:, None, :], axis=0)
        selected = gathered[:, pml_rows]
        projected = (
            jnp.einsum("kij,js->kis", real_blocks, selected, precision=HIGHEST)
            * pml_weight[:, None, :]
        )
        pml_terms = jnp.einsum("kji,kjs->is", real_blocks, projected, precision=HIGHEST)
        result = result.at[:, pml_rows].add(pml_terms * occupied[None, :])
        spread = jnp.zeros((trace_width, face_count + 6 * border), jnp.float32)
        spread = spread.at[:, elem_map].add(result.reshape(trace_width, 4, elements))
        owned_part = spread[:, :face_count]
        sent_back = trade_faces(spread[:, face_count:].reshape(trace_width, 6, border))
        owned_part = owned_part.at[:, border_faces].add(sent_back)
        applied = SIGMA * direction + owned_part
        energy = lax.psum(jnp.sum(direction * applied), ("gx", "gy", "gz"))
        step_size = norm_now / energy
        solution = solution + step_size * direction
        residual = residual - step_size * applied
        norm_next = residual_sum(residual)
        direction = residual + norm_next / norm_now * direction
        norm_now = norm_next
    return (solution.reshape(right_side.shape), residual.reshape(right_side.shape))


def solution(mesh):
    in_specs = (
        P(None, "gx", "gy", "gz"),
        P(None, "gx", "gy", "gz"),
        P("gx", "gy", "gz"),
        P("gx", "gy", "gz"),
        P(None, "gx", "gy", "gz"),
        P("gx", "gy", "gz"),
        P(None, "gx", "gy", "gz"),
        P(),
    )
    out_specs = (P(None, "gx", "gy", "gz"), P(None, "gx", "gy", "gz"))
    return jax.shard_map(local, mesh=mesh, in_specs=in_specs, out_specs=out_specs, check_vma=False)
```

profile of v0, /device:TPU:1, one launch (start us, length us, event | category | flops | bytes accessed | tf_op | source)
XLA Modules:
  0.0 1032.6 jit_solution(6055921485620125392)
XLA Ops:
  7.9 4.6 collective-permute-start
  12.5 5.5 collective-permute-start.1
  28.1 4.2 maximum_bitcast_fusion.1
  34.5 4.7 maximum_bitcast_fusion
  39.2 15.8 %copy.142 = f32[2,3,2,20,4,2,20,4]{7,6,5,4,3,2,1,0:T(8,128)} copy(f32[2,3,2,20,4,2,20,4]{6,7,3,4,0,1,5,2:T(4,128)} %maximum_bitcast_fusion) | data formatting | bytes 1228800 | tf_op jit(solution)/shard_map/transpose | solution.py:36
  55.0 14.2 %reshape_reshape.3 = f32[2,3,160,160]{3,2,1,0:T(8,128)S(1)} reshape(f32[2,3,2,20,4,2,20,4]{7,6,5,4,3,2,1,0:T(8,128)} %copy.142) | data formatting | bytes 1228800 | tf_op jit(solution)/shard_map/reshape;reshape | solution.py:75
  72.7 14.2 %reshape.302 = f32[6,160,160]{2,1,0:T(8,128)S(1)} reshape(f32[2,3,2,20,4,2,20,4]{7,6,5,4,3,2,1,0:T(8,128)} %copy.142) | data formatting | bytes 1228800 | tf_op jit(solution)/shard_map/reshape | solution.py:37
  87.3 2.8 gather_fusion.1
  95.2 6.1 scatter_custom_fusion.3
  101.4 4.2 collective-permute-start.6
  107.5 4.3 collective-permute-start.8
  113.1 4.3 collective-permute-start.10
  118.8 3.4 collective-permute-done.11
  122.3 2.7 scatter_fusion.1
  125.7 112.6 %all-reduce = (f32[]{:T(128)}, f32[]{:T(128)}) all-reduce(f32[]{:T(128)} %get-tuple-element.13, f32[]{:T(128)} %get-tuple-element.12), channel_id=1, replica_groups=mesh['gx'=8,'gy'=4,'gz'=16] {'gx','gy','gz'}, use_global_device_ids=true, to_apply=%region_1.2 | all-reduce | flops 2 | bytes 16 | tf_op jit(solution)/shard_map/psum | solution.py:58
  240.3 99.6 %psum.58 = f32[]{:T(128)} all-reduce(f32[]{:T(128)} %multiply_reduce_fusion.5), channel_id=1, replica_groups=mesh['gx'=8,'gy'=4,'gz'=16] {'gx','gy','gz'}, use_global_device_ids=true, to_apply=%region_13.14 | all-reduce | flops 1 | bytes 8 | tf_op jit(solution)/shard_map/psum | solution.py:58
  342.6 3.3 collective-permute-start.12
  351.0 3.6 collective-permute-start.16
  356.0 3.2 collective-permute-done.17
  359.5 2.8 gather_fusion.5
  367.4 6.1 scatter_custom_fusion.6
  373.6 4.9 collective-permute-start.18
  380.4 4.3 collective-permute-start.20
  389.6 2.7 collective-permute-done.23
  392.3 2.7 scatter_fusion.3
  395.7 105.7 %psum.59 = f32[]{:T(128)} all-reduce(f32[]{:T(128)} %multiply_reduce_fusion.4), channel_id=1, replica_groups=mesh['gx'=8,'gy'=4,'gz'=16] {'gx','gy','gz'}, use_global_device_ids=true, to_apply=%region_19.20 | all-reduce | flops 1 | bytes 8 | tf_op jit(solution)/shard_map/psum | solution.py:119
  503.4 98.6 %psum.60 = f32[]{:T(128)} all-reduce(f32[]{:T(128)} %get-tuple-element.18), channel_id=1, replica_groups=mesh['gx'=8,'gy'=4,'gz'=16] {'gx','gy','gz'}, use_global_device_ids=true, to_apply=%region_21.22 | all-reduce | flops 1 | bytes 8 | tf_op jit(solution)/shard_map/psum | solution.py:58
  604.8 3.1 collective-permute-start.24
  613.0 3.7 collective-permute-start.28
  618.2 3.0 collective-permute-done.29
  621.5 2.8 gather_fusion.8
  630.3 6.5 scatter_custom_fusion.9
  636.9 4.9 collective-permute-start.30
  643.8 4.3 collective-permute-start.32
  652.9 2.7 collective-permute-done.35
  655.7 2.7 scatter_fusion.5
  659.1 105.7 %psum.61 = f32[]{:T(128)} all-reduce(f32[]{:T(128)} %multiply_reduce_fusion.2), channel_id=1, replica_groups=mesh['gx'=8,'gy'=4,'gz'=16] {'gx','gy','gz'}, use_global_device_ids=true, to_apply=%region_27.28 | all-reduce | flops 1 | bytes 8 | tf_op jit(solution)/shard_map/psum | solution.py:119
  766.8 98.6 %psum.62 = f32[]{:T(128)} all-reduce(f32[]{:T(128)} %get-tuple-element.16), channel_id=1, replica_groups=mesh['gx'=8,'gy'=4,'gz'=16] {'gx','gy','gz'}, use_global_device_ids=true, to_apply=%region_29.30 | all-reduce | flops 1 | bytes 8 | tf_op jit(solution)/shard_map/psum | solution.py:58
  868.1 3.2 collective-permute-start.36
  876.5 3.7 collective-permute-start.40
  881.8 2.9 collective-permute-done.41
  885.1 4.0 gather_fusion.11
  895.2 6.1 scatter_custom_fusion.12
  901.4 4.9 collective-permute-start.42
  908.3 4.3 collective-permute-start.44
  917.4 2.7 collective-permute-done.47
  920.2 2.7 scatter_fusion.7
  923.6 105.6 %psum.63 = f32[]{:T(128)} all-reduce(f32[]{:T(128)} %multiply_reduce_fusion), channel_id=1, replica_groups=mesh['gx'=8,'gy'=4,'gz'=16] {'gx','gy','gz'}, use_global_device_ids=true, to_apply=%region_35.36 | all-reduce | flops 1 | bytes 8 | tf_op jit(solution)/shard_map/psum | solution.py:119
  (254 shorter events, 101.2 us)
Async XLA Ops:
  7.9 61.2 %collective-permute-start = (f32[40,1,64]{2,1,0:T(1,128)}, f32[40,1,64]{2,1,0:T(1,128)S(1)}, u32[]{:S(2)}, u32[]{:S(2)}) collective-permute-start(f32[40,1,64]{2,1,0:T(1,128)} %get-tuple-element.71), channel_id=1, source_target_pairs={{0,64},{64,128},{128,192},{192,256},{256,320},{320,384},{384,448},... | collective-permute-start | bytes 30728 | tf_op jit(solution)/shard_map/ppermute | solution.py:22
  12.5 74.5 %collective-permute-start.1 = (f32[40,1,64]{2,1,0:T(1,128)}, f32[40,1,64]{2,1,0:T(1,128)S(1)}, u32[]{:S(2)}, u32[]{:S(2)}) collective-permute-start(f32[40,1,64]{2,1,0:T(1,128)} %get-tuple-element.70), channel_id=1, source_target_pairs={{64,0},{128,64},{192,128},{256,192},{320,256},{384,320},{448,384},... | collective-permute-start | bytes 30728 | tf_op jit(solution)/shard_map/ppermute | solution.py:23
  18.0 69.0 %collective-permute-start.2 = (f32[40,1,64]{2,1,0:T(1,128)}, f32[40,1,64]{2,1,0:T(1,128)S(1)}, u32[]{:S(2)}, u32[]{:S(2)}) collective-permute-start(f32[40,1,64]{2,1,0:T(1,128)} %get-tuple-element.69), channel_id=1, source_target_pairs={{0,16},{16,32},{32,48},{1,17},{17,33},{33,49},{2,18},{18,34},{34,5... | collective-permute-start | bytes 30728 | tf_op jit(solution)/shard_map/ppermute | solution.py:22
  19.3 67.7 %collective-permute-start.3 = (f32[40,1,64]{2,1,0:T(1,128)}, f32[40,1,64]{2,1,0:T(1,128)S(1)}, u32[]{:S(2)}, u32[]{:S(2)}) collective-permute-start(f32[40,1,64]{2,1,0:T(1,128)} %get-tuple-element.68), channel_id=1, source_target_pairs={{16,0},{32,16},{48,32},{17,1},{33,17},{49,33},{18,2},{34,18},{50,3... | collective-permute-start | bytes 30728 | tf_op jit(solution)/shard_map/ppermute | solution.py:23
  20.6 66.4 %collective-permute-start.4 = (f32[40,1,64]{2,1,0:T(1,128)S(1)}, f32[40,1,64]{2,1,0:T(1,128)S(1)}, u32[]{:S(2)}, u32[]{:S(2)}) collective-permute-start(f32[40,1,64]{2,1,0:T(1,128)S(1)} %get-tuple-element.67), channel_id=1, source_target_pairs={{0,1},{1,2},{2,3},{3,4},{4,5},{5,6},{6,7},{7,8},{8,9},{9,10},{10,1... | collective-permute-start | bytes 30728 | tf_op jit(solution)/shard_map/ppermute | solution.py:22
  69.1 17.8 %collective-permute-start.5 = (f32[40,1,64]{2,1,0:T(1,128)S(1)}, f32[40,1,64]{2,1,0:T(1,128)S(1)}, u32[]{:S(2)}, u32[]{:S(2)}) collective-permute-start(f32[40,1,64]{2,1,0:T(1,128)S(1)} %get-tuple-element.66), channel_id=1, source_target_pairs={{1,0},{2,1},{3,2},{4,3},{5,4},{6,5},{7,6},{8,7},{9,8},{10,9},{11,1... | collective-permute-start | bytes 30728 | tf_op jit(solution)/shard_map/ppermute | solution.py:23
  101.4 16.0 %collective-permute-start.6 = (f32[40,1,64]{0,2,1:T(8,128)S(1)}, f32[40,1,64]{0,2,1:T(8,128)S(1)}, u32[]{:S(2)}, u32[]{:S(2)}) collective-permute-start(f32[40,1,64]{0,2,1:T(8,128)S(1)} %get-tuple-element.47), channel_id=1, source_target_pairs={{0,64},{64,128},{128,192},{192,256},{256,320},{320,384},{384,448},... | collective-permute-start | bytes 30728 | tf_op jit(solution)/shard_map/ppermute | solution.py:22
  105.6 13.1 %collective-permute-start.7 = (f32[40,1,64]{0,2,1:T(8,128)S(1)}, f32[40,1,64]{0,2,1:T(8,128)S(1)}, u32[]{:S(2)}, u32[]{:S(2)}) collective-permute-start(f32[40,1,64]{0,2,1:T(8,128)S(1)} %get-tuple-element.46), channel_id=1, source_target_pairs={{64,0},{128,64},{192,128},{256,192},{320,256},{384,320},{448,384},... | collective-permute-start | bytes 30728 | tf_op jit(solution)/shard_map/ppermute | solution.py:23
  107.5 11.2 %collective-permute-start.8 = (f32[40,1,64]{0,2,1:T(8,128)S(1)}, f32[40,1,64]{0,2,1:T(8,128)S(1)}, u32[]{:S(2)}, u32[]{:S(2)}) collective-permute-start(f32[40,1,64]{0,2,1:T(8,128)S(1)} %get-tuple-element.45), channel_id=1, source_target_pairs={{0,16},{16,32},{32,48},{1,17},{17,33},{33,49},{2,18},{18,34},{34,5... | collective-permute-start | bytes 30728 | tf_op jit(solution)/shard_map/ppermute | solution.py:22
  111.8 7.0 collective-permute-start.9
  113.1 5.7 collective-permute-start.10
  117.4 4.9 collective-permute-start.11
  342.6 12.1 %collective-permute-start.12 = (f32[40,1,64]{2,1,0:T(1,128)S(1)}, f32[40,1,64]{2,1,0:T(1,128)S(1)}, u32[]{:S(2)}, u32[]{:S(2)}) collective-permute-start(f32[40,1,64]{2,1,0:T(1,128)S(1)} %get-tuple-element.65), channel_id=1, source_target_pairs={{0,64},{64,128},{128,192},{192,256},{256,320},{320,384},{384,448},... | collective-permute-start | bytes 30728 | tf_op jit(solution)/shard_map/ppermute | solution.py:22
  345.9 10.0 collective-permute-start.13
  347.8 8.1 collective-permute-start.14
  349.7 6.3 collective-permute-start.15
  351.0 5.0 collective-permute-start.16
  354.7 4.5 collective-permute-start.17
  373.6 14.1 %collective-permute-start.18 = (f32[40,1,64]{0,2,1:T(8,128)S(1)}, f32[40,1,64]{0,2,1:T(8,128)S(1)}, u32[]{:S(2)}, u32[]{:S(2)}) collective-permute-start(f32[40,1,64]{0,2,1:T(8,128)S(1)} %get-tuple-element.41), channel_id=1, source_target_pairs={{0,64},{64,128},{128,192},{192,256},{256,320},{320,384},{384,448},... | collective-permute-start | bytes 30728 | tf_op jit(solution)/shard_map/ppermute | solution.py:22
  378.5 10.5 %collective-permute-start.19 = (f32[40,1,64]{0,2,1:T(8,128)S(1)}, f32[40,1,64]{0,2,1:T(8,128)S(1)}, u32[]{:S(2)}, u32[]{:S(2)}) collective-permute-start(f32[40,1,64]{0,2,1:T(8,128)S(1)} %get-tuple-element.40), channel_id=1, source_target_pairs={{64,0},{128,64},{192,128},{256,192},{320,256},{384,320},{448,384},... | collective-permute-start | bytes 30728 | tf_op jit(solution)/shard_map/ppermute | solution.py:23
  380.4 8.6 collective-permute-start.20
  384.7 4.9 collective-permute-start.21
  386.0 3.6 collective-permute-start.22
  387.7 4.7 collective-permute-start.23
  604.8 11.9 %collective-permute-start.24 = (f32[40,1,64]{2,1,0:T(1,128)S(1)}, f32[40,1,64]{2,1,0:T(1,128)S(1)}, u32[]{:S(2)}, u32[]{:S(2)}) collective-permute-start(f32[40,1,64]{2,1,0:T(1,128)S(1)} %get-tuple-element.59), channel_id=1, source_target_pairs={{0,64},{64,128},{128,192},{192,256},{256,320},{320,384},{384,448},... | collective-permute-start | bytes 30728 | tf_op jit(solution)/shard_map/ppermute | solution.py:22
  607.8 10.3 collective-permute-start.25
  609.8 8.4 collective-permute-start.26
  611.7 6.5 collective-permute-start.27
  613.0 5.2 collective-permute-start.28
  616.7 4.5 collective-permute-start.29
  636.9 14.1 %collective-permute-start.30 = (f32[40,1,64]{0,2,1:T(8,128)S(1)}, f32[40,1,64]{0,2,1:T(8,128)S(1)}, u32[]{:S(2)}, u32[]{:S(2)}) collective-permute-start(f32[40,1,64]{0,2,1:T(8,128)S(1)} %get-tuple-element.35), channel_id=1, source_target_pairs={{0,64},{64,128},{128,192},{192,256},{256,320},{320,384},{384,448},... | collective-permute-start | bytes 30728 | tf_op jit(solution)/shard_map/ppermute | solution.py:22
  641.8 10.5 %collective-permute-start.31 = (f32[40,1,64]{0,2,1:T(8,128)S(1)}, f32[40,1,64]{0,2,1:T(8,128)S(1)}, u32[]{:S(2)}, u32[]{:S(2)}) collective-permute-start(f32[40,1,64]{0,2,1:T(8,128)S(1)} %get-tuple-element.34), channel_id=1, source_target_pairs={{64,0},{128,64},{192,128},{256,192},{320,256},{384,320},{448,384},... | collective-permute-start | bytes 30728 | tf_op jit(solution)/shard_map/ppermute | solution.py:23
  643.8 8.6 collective-permute-start.32
  648.0 4.9 collective-permute-start.33
  649.3 3.6 collective-permute-start.34
  651.0 4.7 collective-permute-start.35
  868.1 12.0 %collective-permute-start.36 = (f32[40,1,64]{2,1,0:T(1,128)S(1)}, f32[40,1,64]{2,1,0:T(1,128)S(1)}, u32[]{:S(2)}, u32[]{:S(2)}) collective-permute-start(f32[40,1,64]{2,1,0:T(1,128)S(1)} %get-tuple-element.53), channel_id=1, source_target_pairs={{0,64},{64,128},{128,192},{192,256},{256,320},{320,384},{384,448},... | collective-permute-start | bytes 30728 | tf_op jit(solution)/shard_map/ppermute | solution.py:22
  871.4 10.4 %collective-permute-start.37 = (f32[40,1,64]{2,1,0:T(1,128)S(1)}, f32[40,1,64]{2,1,0:T(1,128)S(1)}, u32[]{:S(2)}, u32[]{:S(2)}) collective-permute-start(f32[40,1,64]{2,1,0:T(1,128)S(1)} %get-tuple-element.52), channel_id=1, source_target_pairs={{64,0},{128,64},{192,128},{256,192},{320,256},{384,320},{448,384},... | collective-permute-start | bytes 30728 | tf_op jit(solution)/shard_map/ppermute | solution.py:23
  873.3 8.4 collective-permute-start.38
  875.2 6.6 collective-permute-start.39
  876.5 5.3 collective-permute-start.40
  880.2 4.5 collective-permute-start.41
  901.4 14.1 %collective-permute-start.42 = (f32[40,1,64]{0,2,1:T(8,128)S(1)}, f32[40,1,64]{0,2,1:T(8,128)S(1)}, u32[]{:S(2)}, u32[]{:S(2)}) collective-permute-start(f32[40,1,64]{0,2,1:T(8,128)S(1)} %get-tuple-element.29), channel_id=1, source_target_pairs={{0,64},{64,128},{128,192},{192,256},{256,320},{320,384},{384,448},... | collective-permute-start | bytes 30728 | tf_op jit(solution)/shard_map/ppermute | solution.py:22
  906.3 10.5 %collective-permute-start.43 = (f32[40,1,64]{0,2,1:T(8,128)S(1)}, f32[40,1,64]{0,2,1:T(8,128)S(1)}, u32[]{:S(2)}, u32[]{:S(2)}) collective-permute-start(f32[40,1,64]{0,2,1:T(8,128)S(1)} %get-tuple-element.28), channel_id=1, source_target_pairs={{64,0},{128,64},{192,128},{256,192},{320,256},{384,320},{448,384},... | collective-permute-start | bytes 30728 | tf_op jit(solution)/shard_map/ppermute | solution.py:23
  908.3 8.6 collective-permute-start.44
  912.5 4.9 collective-permute-start.45
  913.8 3.6 collective-permute-start.46
  915.5 4.7 collective-permute-start.47
  (11 other events, 1110.6 us)
where the time goes:
time: 1040 us; the launch traced here: 1030 us
  blocking collectives  726 us (70%)
  starting transfers between devices  119 us (11%)
  local copies, waits for them, and re-layouts  83.1 us (8%)
  other arithmetic  58 us (6%)
  waiting for transfers between devices  22.5 us (2%)
  between operations  12.3 us (1%)
  matrix products  10.9 us (1%)
    psum x4, blocking collectives, residual_sum(): return lax.psum(jnp.sum(residual * residual), ('gx', 'gy', 'gz'))  409 us
    psum x3, blocking collectives, local(): energy = lax.psum(jnp.sum(direction * applied), ('gx', 'gy', 'gz'))  317 us
    ppermute x24, starting transfers between devices, with_halo(): before = lax.ppermute(last, axis, up)  79 us
    ppermute x24, starting transfers between devices, with_halo(): after = lax.ppermute(first, axis, down)  40.5 us
    scatter-add x4, other arithmetic, local(): spread.at[:, elem_map].add(result.reshape(trace_width, 4, elements))  24.9 us
    ppermute x24, waiting for transfers between devices, with_halo(): after = lax.ppermute(first, axis, down)  22.4 us
  transfers between devices with their start and end apart: 48, of which 10 were waited for; matrix products, arithmetic and copies ran while one was open for 6% of the time, Pallas kernels for 0%

commit v1 on v0

v1 whole, which is shorter than its diff:
```python
import functools

import jax
import jax.numpy as jnp
import numpy as np
from jax import lax
from jax.experimental import pallas as pl
from jax.experimental.pallas import tpu as pltpu
from jax.sharding import PartitionSpec as P

MESH = pl.DeviceIdType.MESH
F32 = jnp.float32
BF16 = jnp.bfloat16
N_GX, N_GY, N_GZ = 8, 4, 16
AXES = (("gx", N_GX), ("gy", N_GY), ("gz", N_GZ))
PLANE = N_GX * N_GY
THETA = 4096.0
SHIFT = 1.75
LANES = 128


def dot(a, b):
    return jnp.dot(a, b, preferred_element_type=F32)


def dot_nt(a, b):
    return lax.dot_general(a, b, (((1,), (1,)), ((), ())), preferred_element_type=F32)


def pieces(value, count):
    out = []
    for _ in range(count):
        head = value.astype(BF16).astype(F32)
        out.append(head)
        value = value - head
    return out


def onehot(left, right):
    return jnp.where(left == right, 1.0, 0.0).astype(BF16)


def embed_matrix():
    out = np.zeros((256, 1024), np.float32)
    for j in range(80):
        face, unknown = divmod(j, 20)
        for part in range(2):
            column = 512 * part + 40 * face + 20 * part + unknown
            out[j, column] = 1.0
            out[j, column + 160] = 1.0
            out[128 + j, column + 320] = 1.0
    return out


def kernel(
    rhs_ref,
    faces_ref,
    class_ref,
    scale_ref,
    stretch_ref,
    flag_ref,
    send_ref,
    blocks_ref,
    embed_ref,
    sol_ref,
    res_ref,
    place,
    pick,
    raw,
    smat,
    smat_t,
    rows,
    zhi,
    zlo,
    part,
    inbox,
    plane_buf,
    line_buf,
    halo_send,
    halo_recv,
    plane_send,
    plane_recv,
    line_send,
    line_recv,
):
    at = {name: lax.axis_index(name) for name, _ in AXES}
    size = dict(AXES)

    def device(**moved):
        return tuple(moved.get(name, at[name]) for name, _ in AXES)

    neighbours, exists = [], []
    for name, n in AXES:
        neighbours.append(device(**{name: lax.rem(at[name] + (n - 1), n)}))
        neighbours.append(device(**{name: lax.rem(at[name] + 1, n)}))
        exists.append(at[name] > 0)
        exists.append(at[name] < n - 1)
    plane_at = at["gx"] * N_GY + at["gy"]
    plane_devices = []
    for step in range(1, PLANE):
        other = lax.rem(plane_at + step, PLANE)
        plane_devices.append(device(gx=other // N_GY, gy=lax.rem(other, N_GY)))
    line_devices = []
    for step in sorted(range(1, N_GZ), key=lambda d: -min(d, N_GZ - d)):
        line_devices.append(device(gz=lax.rem(at["gz"] + step, N_GZ)))

    barrier = pltpu.get_barrier_semaphore()
    for other in plane_devices + line_devices:
        pl.semaphore_signal(barrier, inc=1, device_id=other, device_id_type=MESH)

    sends = []

    def send_halo(step):
        for k in range(6):
            copy = pltpu.make_async_remote_copy(
                src_ref=part.at[step, k],
                dst_ref=inbox.at[step, k ^ 1],
                send_sem=halo_send.at[step, k],
                recv_sem=halo_recv.at[step, k ^ 1],
                device_id=neighbours[k],
                device_id_type=MESH,
            )
            copy.start()
            sends.append(copy)

    lane40 = lax.broadcasted_iota(jnp.int32, (40, LANES), 1)
    own_half = lane40 < 64

    def finish_halo(step, base):
        out = []
        for k in range(6):
            pltpu.make_async_copy(inbox.at[step, k], inbox.at[step, k], halo_recv.at[step, k]).wait()
            mine, got = part[step, k], pltpu.roll(inbox[step, k], 64, 1)
            total = jnp.where(exists[k], mine + got, jnp.where(own_half, mine, 0.0))
            if base is not None:
                total = base[k] + total
            out.append(total)
        last = part[step, 6]
        out.append(last if base is None else base[6] + last)
        return out

    def start_sum(buf, send_sem, recv_sem, which, slot, others, value):
        buf[which, pl.ds(slot, 1)] = value[None]
        for other in others:
            pltpu.make_async_remote_copy(
                src_ref=buf.at[which, pl.ds(slot, 1)],
                dst_ref=buf.at[which, pl.ds(slot, 1)],
                send_sem=send_sem.at[which],
                recv_sem=recv_sem.at[which],
                device_id=other,
                device_id_type=MESH,
            ).start()

    def wait_all(buf, sem, which, count):
        some = buf.at[which, pl.ds(0, count)]
        pltpu.make_async_copy(some, some, sem.at[which]).wait()

    def start_plane(which, value):
        start_sum(plane_buf, plane_send, plane_recv, which, plane_at, plane_devices, value)

    def plane_to_line(which):
        wait_all(plane_buf, plane_recv, which, PLANE - 1)
        value = jnp.sum(plane_buf[which].reshape(PLANE, LANES), axis=0, keepdims=True)
        start_sum(line_buf, line_send, line_recv, which, at["gz"], line_devices, value)

    def finish_line(which):
        wait_all(line_buf, line_recv, which, N_GZ - 1)
        return jnp.sum(line_buf[which].reshape(N_GZ, LANES), axis=0, keepdims=True)

    position = lax.broadcasted_iota(jnp.int32, (1, 384), 1)
    target = ((position // 64) * 128 + position % 64 + 1).astype(F32)
    face_col = lax.broadcasted_iota(jnp.int32, (512, 1), 0)
    sent = jnp.concatenate([send_ref[0:1, :], send_ref[1:2, :], send_ref[2:3, :]], axis=1)
    found = jnp.sum(jnp.where(face_col == sent, target, 0.0), axis=1, keepdims=True)
    inner = jnp.broadcast_to(jnp.where(found > 0.0, 0.0, 1.0), (512, LANES)).astype(BF16)
    below = jnp.where(
        lax.broadcasted_iota(jnp.int32, (512, 512), 1) < lax.broadcasted_iota(jnp.int32, (512, 512), 0), 1.0, 0.0
    ).astype(BF16)
    rank = dot(below, inner)
    new_place = jnp.where(jnp.broadcast_to(found, (512, LANES)) > 0.0, found - 1.0, 768.0 + rank)
    new_int = new_place.astype(jnp.int32)
    lane512 = lax.broadcasted_iota(jnp.int32, (512, LANES), 1)
    for t in range(7):
        place[:, LANES * t : LANES * (t + 1)] = onehot(new_int, lane512 + LANES * t)

    rhs = rhs_ref[...]
    placed = dot(jnp.concatenate(pieces(rhs, 3), axis=0).astype(BF16), place[...])
    placed = placed[0:40] + placed[40:80] + placed[80:120]
    for t in range(7):
        part[0, t] = placed[:, LANES * t : LANES * (t + 1)]
    pl.semaphore_wait(barrier, len(plane_devices) + len(line_devices))
    send_halo(0)

    place_row = new_place.T[0:8, :]
    high = jnp.floor(place_row * (1.0 / 32.0))
    digits = jnp.concatenate([high, place_row - 32.0 * high], axis=0).astype(BF16)
    row512 = lax.broadcasted_iota(jnp.int32, (512, 256), 0)
    row128 = lax.broadcasted_iota(jnp.int32, (LANES, 256), 0)
    for f in range(4):
        old = faces_ref[f : f + 1, :]
        looked = dot(digits, onehot(row512, old))
        owned = (looked[0:1] * 32.0 + looked[8:9]).astype(jnp.int32)
        slot = old - 512
        new = jnp.where(old < 512, owned, (slot // 64) * 128 + 64 + slot % 64)
        for t in range(7):
            pick[LANES * t : LANES * (t + 1), 256 * f : 256 * (f + 1)] = onehot(row128 + LANES * t, new)

    for k in range(8):
        piece = blocks_ref[:, 80 * k : 80 * k + 80]
        rows[pl.ds(k, 120, stride=8), :] = jnp.concatenate([piece, jnp.zeros((120, 48), F32)], axis=1)
    for b in range(6):
        both = jnp.concatenate(pieces(rows[160 * b : 160 * b + 160, :], 2), axis=1).astype(BF16)
        spread = dot(both, embed_ref[...])
        real, imag = spread[0:80], spread[80:160]
        block = jnp.concatenate([real[:, :512] - imag[:, 512:], imag[:, :512] + real[:, 512:]], axis=0)
        raw[160 * b : 160 * b + 160, :] = block
        smat[160 * b : 160 * b + 160, :] = block.astype(BF16)
    raw[960:1024, :] = jnp.zeros((64, 512), F32)
    smat_t[0:160, :] = raw[:, 0:256].T[0:160].astype(BF16)
    smat_t[160:320, :] = raw[:, 256:512].T[64:224].astype(BF16)
    zhi[960:1024, :] = jnp.zeros((64, 256), BF16)
    zlo[960:1024, :] = jnp.zeros((64, 256), BF16)
    weights = []
    for c in range(2):
        for d in range(3):
            factor = jnp.where(flag_ref[...] > 0, stretch_ref[d : d + 1, :], 1.0)
            weights.append(jnp.where(class_ref[...] == c, scale_ref[...] * factor, 0.0))

    def first_half(tiles):
        split = pieces(jnp.concatenate(tiles, axis=1), 2)
        picked = dot(jnp.concatenate(split, axis=0).astype(BF16), pick[...])
        upper = [picked[0:40, 256 * f : 256 * f + 256] for f in range(4)]
        lower = [picked[40:80, 256 * f : 256 * f + 256] for f in range(4)]
        stacked = jnp.concatenate(upper + lower + upper + [jnp.zeros((32, 256), F32)], axis=0).astype(BF16)
        energy = jnp.zeros((8, 256), F32)
        for b in range(6):
            projected = dot(smat[160 * b : 160 * b + 160, :], stacked)
            weighted = projected * weights[b]
            energy = energy + jnp.sum((weighted * projected).reshape(20, 8, 256), axis=0)
            head, tail = pieces(weighted, 2)
            zhi[160 * b : 160 * b + 160, :] = head.astype(BF16)
            zlo[160 * b : 160 * b + 160, :] = tail.astype(BF16)
        return energy

    def second_half(step):
        both = dot(smat_t[...], zhi[...])
        image = both[0:160] + both[160:320] + dot(smat_t[0:160, :], zlo[...])
        wide = jnp.concatenate([image[40 * f : 40 * f + 40] for f in range(4)], axis=1)
        spread = dot_nt(jnp.concatenate(pieces(wide, 3), axis=0).astype(BF16), pick[...])
        spread = spread[0:40] + spread[40:80] + spread[80:120]
        for t in range(7):
            part[step, t] = spread[:, LANES * t : LANES * (t + 1)]
        send_halo(step)

    def own(tiles):
        return [jnp.where(own_half, x, 0.0) for x in tiles[:6]] + [tiles[6]]

    def product(mine, tiles):
        total = mine[0] * tiles[0]
        for t in range(1, 7):
            total = total + mine[t] * tiles[t]
        return jnp.sum(total, axis=0, keepdims=True)

    def energy_row(energy):
        row = jnp.sum(energy, axis=0, keepdims=True)
        return row[:, 0:128] + row[:, 128:256]

    def to_lanes(lines):
        square = jnp.concatenate(lines + [jnp.zeros((16 - len(lines), LANES), F32)], axis=0)
        sums = jnp.sum(square, axis=1, keepdims=True)
        on_diagonal = lax.broadcasted_iota(jnp.int32, (16, LANES), 0) == lax.broadcasted_iota(jnp.int32, (16, LANES), 1)
        return jnp.sum(jnp.where(on_diagonal, sums, 0.0), axis=0, keepdims=True)

    def scalar(line, q):
        return jnp.broadcast_to(line[:, q : q + 1], (1, LANES))

    def combine(terms):
        total = None
        for factor, value in terms:
            total = factor * value if total is None else total + factor * value
        return total

    def lincomb(*terms):
        return [combine([(factor, tiles[t]) for factor, tiles in terms]) for t in range(7)]

    def back(tiles_list):
        stack = []
        for tiles in tiles_list:
            stack += pieces(jnp.concatenate(tiles, axis=1), 3)
        moved = dot_nt(jnp.concatenate(stack, axis=0).astype(BF16), place[...])
        out = []
        for i in range(len(tiles_list)):
            out.append(moved[120 * i : 120 * i + 40] + moved[120 * i + 40 : 120 * i + 80] + moved[120 * i + 80 : 120 * i + 120])
        return out

    first = finish_halo(0, None)
    energy = first_half(first)
    norm_row = product(own(first), first)
    start_plane(0, to_lanes([norm_row, norm_row + energy_row(energy)]))
    second_half(1)
    plane_to_line(0)
    image1 = finish_halo(1, first)
    first_half(image1)
    second_half(2)
    totals = finish_line(0)
    image2 = finish_halo(2, image1)

    norm0, curve0 = scalar(totals, 0), scalar(totals, 1)
    alpha0 = norm0 / curve0
    rho = SHIFT * curve0 / norm0
    eta = 1.0 / jnp.sqrt(norm0)
    inv_eta = 1.0 / eta
    inv_theta = 1.0 / THETA

    unit = lincomb((eta, first))
    res1 = lincomb((eta, first), (-eta * alpha0, image1))
    krylov1 = lincomb((eta * inv_theta, image1), (-eta * alpha0 * inv_theta, image2), (-rho * inv_theta, res1))
    first_half(krylov1)
    second_half(3)
    image3 = finish_halo(3, krylov1)
    krylov2 = lincomb((inv_theta, image3), (-rho * inv_theta, krylov1))

    energy = first_half(krylov2)
    basis = [unit, res1, krylov1, krylov2]
    masked = [own(tiles) for tiles in basis]
    pairs = [(0, 1), (0, 2), (0, 3), (1, 1), (1, 2), (1, 3), (2, 2), (2, 3), (3, 3)]
    lines = [product(masked[i], basis[j]) for i, j in pairs]
    start_plane(1, to_lanes(lines + [lines[-1] + energy_row(energy)]))
    second_half(4)
    plane_to_line(1)
    res1_own, krylov1_own, krylov2_own = back([res1, krylov1, krylov2])
    image4 = finish_halo(4, krylov2)
    krylov3_own = back([lincomb((inv_theta, image4), (-rho * inv_theta, krylov2))])[0]
    totals = finish_line(1)

    gram = {(0, 0): eta * eta * norm0}
    for q, (i, j) in enumerate(pairs):
        gram[i, j] = gram[j, i] = scalar(totals, q)
    inv_alpha0 = 1.0 / alpha0
    gram[3, 4] = (scalar(totals, 9) - rho * gram[3, 3]) * inv_theta
    gram[2, 4] = gram[3, 3]
    gram[1, 4] = gram[2, 3]
    gram[0, 4] = ((gram[0, 3] - gram[1, 3]) * inv_alpha0 - rho * gram[0, 3]) * inv_theta

    def apply(p):
        scaled = p[0] * inv_alpha0
        out = [scaled, rho * p[1] - scaled]
        for i in range(2, len(p)):
            out.append(rho * p[i] + THETA * p[i - 1])
        return out + [THETA * p[-1]]

    def form(a, b):
        return combine([(x, combine([(y, gram[i, j]) for j, y in enumerate(b)])) for i, x in enumerate(a)])

    norm = gram[1, 1]
    zero = jnp.zeros((1, LANES), F32)
    sol = [alpha0, zero, zero, zero]
    res = [zero, zero + 1.0]
    direction = [norm / gram[0, 0], zero + 1.0]
    for i in range(3):
        image = apply(direction)
        alpha = norm / form(direction, image)
        for j, x in enumerate(direction):
            sol[j] = sol[j] + alpha * x
        res = res + [zero]
        res = [x - alpha * y for x, y in zip(res, image)]
        if i < 2:
            new = form(res, res)
            beta = new / norm
            direction = [x + beta * y for x, y in zip(res, direction + [zero])]
            norm = new

    def wide(line):
        return jnp.concatenate([line] * 4, axis=1)

    sol_ref[...] = combine(
        [
            (wide(sol[0]), rhs),
            (wide(sol[1] * inv_eta), res1_own),
            (wide(sol[2] * inv_eta), krylov1_own),
            (wide(sol[3] * inv_eta), krylov2_own),
        ]
    )
    res_ref[...] = combine(
        [
            (wide(res[0]), rhs),
            (wide(res[1] * inv_eta), res1_own),
            (wide(res[2] * inv_eta), krylov1_own),
            (wide(res[3] * inv_eta), krylov2_own),
            (wide(res[4] * inv_eta), krylov3_own),
        ]
    )
    for copy in sends:
        copy.wait_send()
    for which in range(2):
        wait_all(plane_buf, plane_send, which, PLANE - 1)
        wait_all(line_buf, line_send, which, N_GZ - 1)


def local(right_side, elem_faces, elem_class, elem_scale, stretch, pml_flag, send_faces, blocks):
    vmem = pl.BlockSpec(memory_space=pltpu.VMEM)
    steps = 5
    field = jax.ShapeDtypeStruct((40, 512), F32)
    solution_field, residual = pl.pallas_call(
        kernel,
        out_shape=(field, field),
        in_specs=[vmem] * 9,
        out_specs=(vmem, vmem),
        scratch_shapes=[
            pltpu.VMEM((512, 896), BF16),
            pltpu.VMEM((896, 1024), BF16),
            pltpu.VMEM((1024, 512), F32),
            pltpu.VMEM((960, 512), BF16),
            pltpu.VMEM((320, 1024), BF16),
            pltpu.VMEM((960, LANES), F32),
            pltpu.VMEM((1024, 256), BF16),
            pltpu.VMEM((1024, 256), BF16),
            pltpu.VMEM((steps, 7, 40, LANES), F32),
            pltpu.VMEM((steps, 6, 40, LANES), F32),
            pltpu.VMEM((2, PLANE, 1, LANES), F32),
            pltpu.VMEM((2, N_GZ, 1, LANES), F32),
            pltpu.SemaphoreType.DMA((steps, 6)),
            pltpu.SemaphoreType.DMA((steps, 6)),
            pltpu.SemaphoreType.DMA((2,)),
            pltpu.SemaphoreType.DMA((2,)),
            pltpu.SemaphoreType.DMA((2,)),
            pltpu.SemaphoreType.DMA((2,)),
        ],
        compiler_params=pltpu.CompilerParams(
            collective_id=0, has_side_effects=True, vmem_limit_bytes=40 * 1024 * 1024
        ),
    )(
        right_side.reshape(40, 512),
        elem_faces.reshape(4, 256),
        elem_class.reshape(1, 256),
        elem_scale.reshape(1, 256),
        stretch.reshape(3, 256),
        pml_flag.reshape(1, 256),
        send_faces.reshape(3, 128),
        blocks.reshape(120, 640),
        jnp.asarray(embed_matrix(), BF16),
    )
    return solution_field.reshape(right_side.shape), residual.reshape(right_side.shape)


def solution(mesh):
    in_specs = (
        P(None, "gx", "gy", "gz"),
        P(None, "gx", "gy", "gz"),
        P("gx", "gy", "gz"),
        P("gx", "gy", "gz"),
        P(None, "gx", "gy", "gz"),
        P("gx", "gy", "gz"),
        P(None, "gx", "gy", "gz"),
        P(),
    )
    out_specs = (P(None, "gx", "gy", "gz"), P(None, "gx", "gy", "gz"))
    return jax.shard_map(local, mesh=mesh, in_specs=in_specs, out_specs=out_specs, check_vma=False)
```

time: 1040 us -> 60.2 us (0.06)
  blocking collectives: 726 us -> 0 us
  starting transfers between devices: 119 us -> 0 us
  local copies, waits for them, and re-layouts: 83.1 us -> 5.1 us
  other arithmetic: 58 us -> 0.7 us
  Pallas kernels: 0 us -> 53.4 us
  waiting for transfers between devices: 22.5 us -> 0 us
  between operations: 12.3 us -> 0.7 us
  matrix products: 10.9 us -> 0 us
    psum x7 -> x0, blocking collectives: 726 us -> none  [the longest x4 409 us: residual_sum(): return lax.psum(jnp.sum(residual * residual), ('gx', 'gy', 'gz'))]
    ppermute x48 -> x0, starting transfers between devices: 119 us -> none  [the longest x24 79 us: with_halo(): before = lax.ppermute(last, axis, up)]
    pallas_call x0 -> x1, Pallas kernels: none -> 53.4 us  [local(): pl.pallas_call(kernel, out_shape=(field, field), in_specs=[vmem] * 9, out...]
    scatter-add x12 -> x0, other arithmetic: 40.1 us -> none  [the longest x4 24.9 us: local(): spread.at[:, elem_map].add(result.reshape(trace_width, 4, elements))]
    gather x21 -> x0, local copies, waits for them, and re-layouts: 22.7 us -> none  [the longest x8 14.2 us: local(): gathered = extended[:, elem_map].reshape(4 * trace_width, elements)]
    ppermute x48 -> x0, waiting for transfers between devices: 22.5 us -> none  [the longest x24 22.4 us: with_halo(): after = lax.ppermute(first, axis, down)]
    another operation x4 -> x0, local copies, waits for them, and re-layouts: 18 us -> none  [the longest x1 14.2 us: local(): real_blocks.reshape(classes, 3, real_blocks.shape[1], real_blocks.shape[2])]
    reshape x25 -> x2, local copies, waits for them, and re-layouts: 17.4 us -> 1.31 us  [the longest x1 1.24 us: local(): blocks.reshape(120, 640)]
  transfers between devices with their start and end apart: 48 -> 0, of which waited for: 10 -> 0; matrix products, arithmetic and copies ran while one was open for 6% -> 0% of each run, Pallas kernels for 0% -> 0%
where the time goes in v1:
time: 60.2 us; the launch traced here: 59.9 us
  Pallas kernels  53.4 us (89%)
  local copies, waits for them, and re-layouts  5.1 us (8%)
  other arithmetic  0.7 us (1%)
  between operations  0.7 us (1%)
    pallas_call x1, Pallas kernels, local(): pl.pallas_call(kernel, out_shape=(field, field), in_specs=[vmem] * 9, out...  53.4 us
    unnamed x13, local copies, waits for them, and re-layouts  3.78 us
    reshape x1, local copies, waits for them, and re-layouts, local(): blocks.reshape(120, 640)  1.24 us

profile of v1, /device:TPU:1, one launch (start us, length us, event | category | flops | bytes accessed | tf_op | source)
XLA Modules:
  0.0 59.9 jit_solution(16868409992508931355)
XLA Ops:
  0.6 0.0 copy-start
  0.6 0.7 %copy.21 = s32[4,1,1,256]{3,0,1,2:T(4,128)S(1)} copy(s32[4,1,1,256]{3,2,1,0:T(1,128)} %param.10) | data formatting | bytes 8192
  1.4 0.7 %copy.20 = f32[3,1,1,256]{3,0,1,2:T(4,128)S(1)} copy(f32[3,1,1,256]{3,2,1,0:T(1,128)} %param.13) | data formatting | bytes 6144
  2.1 0.7 %reduce = s32[6,64]{1,0:T(8,128)S(1)} reduce(s32[6,1,1,64]{3,2,1,0:T(1,128)} %param.15, s32[]{:T(128)} %constant.10), dimensions={1,2}, to_apply=%param.15.reduce_sub_computation | reduce | bytes 3076 | tf_op args[6]
  2.8 0.1 reshape.40.send_ref
  2.9 0.9 %copy.19 = f32[40,1,1,512]{3,0,1,2:T(8,128)S(1)} copy(f32[40,1,1,512]{3,2,1,0:T(1,128)} %param.9) | data formatting | bytes 163840
  3.7 0.0 copy-start.1
  3.7 0.0 copy-start.2
  3.8 0.0 copy-start.3
  3.8 1.2 %reshape.41.blocks_ref = f32[120,640]{1,0:T(8,128)S(1)} reshape(f32[2,3,2,6400]{3,2,1,0:T(2,128)} %param.16) | data formatting | bytes 614400 | tf_op jit(solution)/shard_map/reshape | solution.py:440
  5.0 0.0 copy-done
  5.0 0.0 copy-done.1
  5.0 0.0 copy-done.2
  5.0 0.0 copy-done.3
  5.0 53.4 %shard_map.104 = (f32[40,512]{1,0:T(8,128)S(1)}, f32[40,512]{1,0:T(8,128)S(1)}) custom-call(f32[40,512]{1,0:T(8,128)S(1)} %bitcast.14, s32[4,256]{1,0:T(4,128)S(1)} %bitcast.18, s32[1,256]{1,0:T(1,128)S(1)} %bitcast.19, f32[1,256]{1,0:T(1,128)S(1)} %bitcast.20, f32[3,256]{1,0:T(4,128)S(1)} %bitcast.17, s32[1,256]{1,0:T(1,128)S(1)} %bitcast.21, ...), custom_call_target="tpu_custom_call" | custom-call | tf_op jit(solution)/shard_map/pallas_call | solution.py:404
  58.5 0.7 %copy.11 = f32[40,1,1,512]{3,2,1,0:T(1,128)} copy(f32[40,1,1,512]{3,0,2,1:T(8,128)S(1)} %bitcast.16) | data formatting | bytes 163840
  59.2 0.7 %copy.12 = f32[40,1,1,512]{3,2,1,0:T(1,128)} copy(f32[40,1,1,512]{3,0,2,1:T(8,128)S(1)} %bitcast.15) | data formatting | bytes 163840
Async XLA Ops:
  0.6 4.4 %copy-start = (bf16[256,1024]{1,0:T(8,128)(2,1)S(1)}, bf16[256,1024]{1,0:T(8,128)(2,1)}, u32[]{:S(2)}) copy-start(bf16[256,1024]{1,0:T(8,128)(2,1)} %constant.2.clone.embed_ref) | copy-start | bytes 1572868
  3.7 1.3 %copy-start.1 = (s32[1,1,256]{2,1,0:T(1,128)S(1)}, s32[1,1,256]{2,1,0:T(1,128)}, u32[]{:S(2)}) copy-start(s32[1,1,256]{2,1,0:T(1,128)} %param.11) | copy-start | bytes 3076
  3.7 1.3 %copy-start.2 = (f32[1,1,256]{2,1,0:T(1,128)S(1)}, f32[1,1,256]{2,1,0:T(1,128)}, u32[]{:S(2)}) copy-start(f32[1,1,256]{2,1,0:T(1,128)} %param.12) | copy-start | bytes 3076
  3.8 1.3 %copy-start.3 = (s32[1,1,256]{2,1,0:T(1,128)S(1)}, s32[1,1,256]{2,1,0:T(1,128)}, u32[]{:S(2)}) copy-start(s32[1,1,256]{2,1,0:T(1,128)} %param.14) | copy-start | bytes 3076

commit v2 on v1

v2 whole, which is shorter than its diff:
```python
import functools

import jax
import jax.numpy as jnp
import numpy as np
from jax import lax
from jax.experimental import pallas as pl
from jax.experimental.pallas import tpu as pltpu
from jax.sharding import PartitionSpec as P

MESH = pl.DeviceIdType.MESH
F32 = jnp.float32
BF16 = jnp.bfloat16
N_GX, N_GY, N_GZ = 8, 4, 16
AXES = (("gx", N_GX), ("gy", N_GY), ("gz", N_GZ))
PLANE = N_GX * N_GY
LANES = 128
EARLY = 640
TILE = (0, 1, 2, 3, 5, 6)
STEPS = 5


def dot(a, b):
    return jnp.dot(a, b, preferred_element_type=F32)


def dot_nt(a, b):
    return lax.dot_general(a, b, (((1,), (1,)), ((), ())), preferred_element_type=F32)


def pieces(value, count):
    out = []
    for _ in range(count):
        head = value.astype(BF16).astype(F32)
        out.append(head)
        value = value - head
    return out


def onehot(left, right):
    return jnp.where(left == right, 1.0, 0.0).astype(BF16)


def embed_rows():
    column = lax.broadcasted_iota(jnp.int32, (1, 1024), 1)
    part, inside = column // 512, column % 512
    copy, place = inside // 160, inside % 160
    face, rest = place // 40, place % 40
    row = face * 20 + rest % 20 + jnp.where(copy == 2, 128, 0)
    return jnp.where((copy < 3) & (rest // 20 == part), row, -1)


def kernel(
    rhs_in,
    faces_in,
    class_in,
    scale_in,
    stretch_in,
    flag_in,
    send_in,
    blocks_in,
    sol_ref,
    res_ref,
    rhs_ref,
    faces_ref,
    class_ref,
    scale_ref,
    stretch_ref,
    flag_ref,
    send_ref,
    blocks_ref,
    lines640,
    embed,
    place,
    pick,
    raw,
    smat,
    smat_t,
    rows,
    zhi,
    zlo,
    part,
    inbox,
    plane_buf,
    line_buf,
    halo_send,
    halo_recv,
    plane_send,
    plane_recv,
    line_send,
    line_recv,
    load_sem,
):
    at = {name: lax.axis_index(name) for name, _ in AXES}
    size = dict(AXES)

    def device(**moved):
        return tuple(moved.get(name, at[name]) for name, _ in AXES)

    neighbours, exists = [], []
    for name, n in AXES:
        neighbours.append(device(**{name: lax.rem(at[name] + (n - 1), n)}))
        neighbours.append(device(**{name: lax.rem(at[name] + 1, n)}))
        exists.append(at[name] > 0)
        exists.append(at[name] < n - 1)
    plane_at = at["gx"] * N_GY + at["gy"]
    offsets = [(dx, dy) for dx in range(N_GX) for dy in range(N_GY) if dx or dy]
    offsets.sort(key=lambda d: -(min(d[0], N_GX - d[0]) // 2 + min(d[1], N_GY - d[1])))
    plane_devices = []
    for dx, dy in offsets:
        plane_devices.append(device(gx=lax.rem(at["gx"] + dx, N_GX), gy=lax.rem(at["gy"] + dy, N_GY)))
    line_devices = []
    for step in sorted(range(1, N_GZ), key=lambda d: -min(d, N_GZ - d)):
        line_devices.append(device(gz=lax.rem(at["gz"] + step, N_GZ)))

    barrier = pltpu.get_barrier_semaphore()
    for other in plane_devices + line_devices:
        pl.semaphore_signal(barrier, inc=1, device_id=other, device_id_type=MESH)

    loads = []
    held = (send_ref, rhs_ref, faces_ref, blocks_ref, class_ref, scale_ref, stretch_ref, flag_ref)
    given = (send_in, rhs_in, faces_in, blocks_in, class_in, scale_in, stretch_in, flag_in)
    for i, (there, here) in enumerate(zip(given, held)):
        copy = pltpu.make_async_copy(there, here, load_sem.at[i])
        copy.start()
        loads.append(copy)

    sends = []

    def send_halo(step, directions):
        for k in directions:
            copy = pltpu.make_async_remote_copy(
                src_ref=part.at[step, TILE[k]],
                dst_ref=inbox.at[step, k ^ 1],
                send_sem=halo_send.at[step, k],
                recv_sem=halo_recv.at[step, k ^ 1],
                device_id=neighbours[k],
                device_id_type=MESH,
            )
            copy.start()
            sends.append(copy)

    lane40 = lax.broadcasted_iota(jnp.int32, (40, LANES), 1)
    own_half = lane40 < 64

    def receive(step, k):
        pltpu.make_async_copy(inbox.at[step, k], inbox.at[step, k], halo_recv.at[step, k]).wait()
        mine, got = part[step, TILE[k]], pltpu.roll(inbox[step, k], 64, 1)
        return jnp.where(exists[k], mine + got, jnp.where(own_half, mine, 0.0))

    def start_sum(buf, send_sem, recv_sem, which, slot, others, value):
        buf[which, pl.ds(slot, 1)] = value[None]
        for other in others:
            pltpu.make_async_remote_copy(
                src_ref=buf.at[which, pl.ds(slot, 1)],
                dst_ref=buf.at[which, pl.ds(slot, 1)],
                send_sem=send_sem.at[which],
                recv_sem=recv_sem.at[which],
                device_id=other,
                device_id_type=MESH,
            ).start()

    def wait_all(buf, sem, which, count):
        some = buf.at[which, pl.ds(0, count)]
        pltpu.make_async_copy(some, some, sem.at[which]).wait()

    def start_plane(which, value):
        start_sum(plane_buf, plane_send, plane_recv, which, plane_at, plane_devices, value)

    def plane_to_line(which):
        wait_all(plane_buf, plane_recv, which, PLANE - 1)
        value = jnp.sum(plane_buf[which], axis=0)
        start_sum(line_buf, line_send, line_recv, which, at["gz"], line_devices, value)

    def finish_line(which):
        wait_all(line_buf, line_recv, which, N_GZ - 1)
        return jnp.sum(line_buf[which], axis=0)

    position = lax.broadcasted_iota(jnp.int32, (1, 384), 1)
    target = ((position // 64) * 128 + jnp.where(position >= 256, 128, 0) + position % 64 + 1).astype(F32)
    face_col = lax.broadcasted_iota(jnp.int32, (512, 1), 0)
    loads[0].wait()
    sent = jnp.concatenate([send_ref[k, 0] for k in range(6)], axis=1)
    found = jnp.sum(jnp.where(face_col == sent, target, 0.0), axis=1, keepdims=True)
    inner = jnp.broadcast_to(jnp.where(found > 0.0, 0.0, 1.0), (512, LANES)).astype(BF16)
    below = jnp.where(
        lax.broadcasted_iota(jnp.int32, (512, 512), 1) < lax.broadcasted_iota(jnp.int32, (512, 512), 0), 1.0, 0.0
    ).astype(BF16)
    rank = dot(below, inner)
    new_place = jnp.where(jnp.broadcast_to(found, (512, LANES)) > 0.0, found - 1.0, 512.0 + rank)
    new_int = new_place.astype(jnp.int32)
    lane512 = lax.broadcasted_iota(jnp.int32, (512, LANES), 1)
    for t in range(7):
        place[:, LANES * t : LANES * (t + 1)] = onehot(new_int, lane512 + LANES * t)

    loads[1].wait()
    rhs = rhs_ref[:, 0, 0, :]
    placed = dot(jnp.concatenate(pieces(rhs, 3), axis=0).astype(BF16), place[...])
    placed = placed[0:40] + placed[40:80] + placed[80:120]
    for t in range(7):
        part[0, t] = placed[:, LANES * t : LANES * (t + 1)]
    pl.semaphore_wait(barrier, len(plane_devices) + len(line_devices))
    send_halo(0, (4, 5, 2, 3, 0, 1))

    place_row = new_place.T[0:8, :]
    high = jnp.floor(place_row * (1.0 / 32.0))
    digits = jnp.concatenate([high, place_row - 32.0 * high], axis=0).astype(BF16)
    row512 = lax.broadcasted_iota(jnp.int32, (512, 256), 0)
    row128 = lax.broadcasted_iota(jnp.int32, (LANES, 256), 0)
    loads[2].wait()
    for f in range(4):
        old = faces_ref[f, 0]
        looked = dot(digits, onehot(row512, old))
        owned = (looked[0:1] * 32.0 + looked[8:9]).astype(jnp.int32)
        slot = old - 512
        new = jnp.where(old < 512, owned, (slot // 64) * 128 + jnp.where(slot >= 256, 128, 0) + 64 + slot % 64)
        for t in range(7):
            pick[LANES * t : LANES * (t + 1), 256 * f : 256 * (f + 1)] = onehot(row128 + LANES * t, new)

    embed[...] = onehot(lax.broadcasted_iota(jnp.int32, (256, 1024), 0), embed_rows())
    loads[3].wait()
    for b in range(6):
        for g in range(10):
            lines640[20 * b + 2 * g : 20 * b + 2 * g + 2, :] = blocks_ref[b // 3, b % 3, :, 640 * g : 640 * g + 640]
    for k in range(8):
        piece = lines640[:, 80 * k : 80 * k + 80]
        rows[pl.ds(k, 120, stride=8), :] = jnp.concatenate([piece, jnp.zeros((120, 48), F32)], axis=1)
    for b in range(6):
        both = jnp.concatenate(pieces(rows[160 * b : 160 * b + 160, :], 2), axis=1).astype(BF16)
        spread = dot(both, embed[...]).reshape(10, 2, 8, 1024)
        real, imag = spread[:, 0].reshape(80, 1024), spread[:, 1].reshape(80, 1024)
        block = jnp.concatenate([real[:, :512] - imag[:, 512:], imag[:, :512] + real[:, 512:]], axis=0)
        raw[160 * b : 160 * b + 160, :] = block
        smat[160 * b : 160 * b + 160, :] = block.astype(BF16)
    raw[960:1024, :] = jnp.zeros((64, 512), F32)
    smat_t[0:160, :] = raw[:, 0:256].T[0:160].astype(BF16)
    smat_t[160:320, :] = raw[:, 256:512].T[64:224].astype(BF16)
    zhi[960:1024, :] = jnp.zeros((64, 256), BF16)
    zlo[960:1024, :] = jnp.zeros((64, 256), BF16)
    for copy in loads[4:]:
        copy.wait()
    weights = []
    for c in range(2):
        for d in range(3):
            factor = jnp.where(flag_ref[0] > 0, stretch_ref[d, 0], 1.0)
            weights.append(jnp.where(class_ref[0] == c, scale_ref[0] * factor, 0.0))

    def gather(tiles, low, high):
        split = pieces(jnp.concatenate(tiles, axis=1), 2)
        return dot(jnp.concatenate(split, axis=0).astype(BF16), pick[low:high, :])

    def project(picked, with_energy):
        upper = [picked[0:40, 256 * f : 256 * f + 256] for f in range(4)]
        lower = [picked[40:80, 256 * f : 256 * f + 256] for f in range(4)]
        stacked = jnp.concatenate(upper + lower + upper + [jnp.zeros((32, 256), F32)], axis=0).astype(BF16)
        energy = jnp.zeros((8, 256), F32)
        for b in range(6):
            projected = dot(smat[160 * b : 160 * b + 160, :], stacked)
            weighted = projected * weights[b]
            if with_energy:
                energy = energy + jnp.sum((weighted * projected).reshape(20, 8, 256), axis=0)
            head, tail = pieces(weighted, 2)
            zhi[160 * b : 160 * b + 160, :] = head.astype(BF16)
            zlo[160 * b : 160 * b + 160, :] = tail.astype(BF16)
        return energy

    def scatter(step):
        both = dot(smat_t[...], zhi[...])
        image = both[0:160] + both[160:320] + dot(smat_t[0:160, :], zlo[...])
        wide = jnp.concatenate([image[40 * f : 40 * f + 40] for f in range(4)], axis=1)
        split = jnp.concatenate(pieces(wide, 3), axis=0).astype(BF16)
        for tiles, directions in (((5, 6), (4, 5)), ((2, 3), (2, 3)), ((0, 1), (0, 1)), ((4,), ())):
            low = LANES * tiles[0]
            spread = dot_nt(split, pick[low : low + LANES * len(tiles), :])
            spread = spread[0:40] + spread[40:80] + spread[80:120]
            for n, t in enumerate(tiles):
                part[step, t] = spread[:, LANES * n : LANES * (n + 1)]
            send_halo(step, directions)

    def own(tiles):
        return [x if t == 4 else jnp.where(own_half, x, 0.0) for t, x in enumerate(tiles)]

    def product(mine, tiles):
        total = mine[0] * tiles[0]
        for t in range(1, 7):
            total = total + mine[t] * tiles[t]
        return jnp.sum(total, axis=0, keepdims=True)

    def energy_row(energy):
        row = jnp.sum(energy, axis=0, keepdims=True)
        return row[:, 0:128] + row[:, 128:256]

    def to_lanes(lines):
        square = jnp.concatenate(lines + [jnp.zeros((16 - len(lines), LANES), F32)], axis=0)
        sums = jnp.sum(square, axis=1, keepdims=True)
        on_diagonal = lax.broadcasted_iota(jnp.int32, (16, LANES), 0) == lax.broadcasted_iota(jnp.int32, (16, LANES), 1)
        return jnp.sum(jnp.where(on_diagonal, sums, 0.0), axis=0, keepdims=True)

    def scalar(line, q):
        return jnp.broadcast_to(line[:, q : q + 1], (1, LANES))

    def combine(terms):
        total = None
        for factor, value in terms:
            total = factor * value if total is None else total + factor * value
        return total

    def back(tiles_list):
        stack = []
        for tiles in tiles_list:
            stack += pieces(jnp.concatenate(tiles, axis=1), 3)
        moved = dot_nt(jnp.concatenate(stack, axis=0).astype(BF16), place[...])
        out = []
        for i in range(len(tiles_list)):
            out.append(moved[120 * i : 120 * i + 40] + moved[120 * i + 40 : 120 * i + 80] + moved[120 * i + 80 : 120 * i + 120])
        return out

    total = blocks_ref[...]
    total = jnp.sum(total * total, axis=(0, 1, 2))
    rho = 1.0 + jnp.sum(total.reshape(1, 6400), axis=1, keepdims=True) * (3.0 / 160.0)
    rho = jnp.broadcast_to(rho, (1, LANES))
    theta = 256.0 * rho
    inv_theta = 1.0 / theta
    keep = (1.0 - rho) * inv_theta

    basis, masked, sums, moved = [], [], {}, [rhs]

    def advance(step):
        def tile(t, got):
            return got if step == 0 else keep * basis[-1][t] + inv_theta * got

        early = [tile(k, receive(step, k)) for k in range(4)] + [tile(4, part[step, 4])]
        picked = gather(early, 0, EARLY) if step < 4 else None
        late = [tile(TILE[k], receive(step, k)) for k in (4, 5)]
        if step < 4:
            picked = picked + gather(late, EARLY, 896)
        basis.append(early + late)
        return picked

    def inner(i, j):
        sums[i, j] = product(masked[i], basis[j])

    for step in range(3):
        project(advance(step), False)
        masked.append(own(basis[step]))
        scatter(step + 1)
        for i in range(step + 1):
            inner(i, step)
        if step:
            moved += back([basis[step]])
    energy = project(advance(3), True)
    masked.append(own(basis[3]))
    for i in range(4):
        inner(i, 3)
    pairs = [(i, j) for i in range(4) for j in range(i, 4)]
    start_plane(0, to_lanes([sums[pair] for pair in pairs] + [sums[3, 3] + energy_row(energy)]))
    scatter(4)
    plane_to_line(0)
    moved += back([basis[3]])
    advance(4)
    moved += back([basis[4]])
    totals = finish_line(0)

    gram = {}
    for q, (i, j) in enumerate(pairs):
        gram[i, j] = gram[j, i] = scalar(totals, q)
    gram[3, 4] = (scalar(totals, len(pairs)) - rho * gram[3, 3]) * inv_theta
    gram[2, 4] = gram[3, 3]
    gram[1, 4] = gram[2, 3]
    gram[0, 4] = gram[1, 3]

    def apply(p):
        out = [rho * p[0]]
        for i in range(1, len(p)):
            out.append(rho * p[i] + theta * p[i - 1])
        return out + [theta * p[-1]]

    def form(a, b):
        return combine([(x, combine([(y, gram[i, j]) for j, y in enumerate(b)])) for i, x in enumerate(a)])

    norm = gram[0, 0]
    zero = jnp.zeros((1, LANES), F32)
    sol, res, direction = [zero] * 4, [zero + 1.0], [zero + 1.0]
    for i in range(4):
        image = apply(direction)
        alpha = norm / form(direction, image)
        for j, x in enumerate(direction):
            sol[j] = sol[j] + alpha * x
        res = [x - alpha * y for x, y in zip(res + [zero], image)]
        if i < 3:
            new = form(res, res)
            beta = new / norm
            direction = [x + beta * y for x, y in zip(res, direction + [zero])]
            norm = new

    def wide(line):
        return jnp.concatenate([line] * 4, axis=1)

    sol_ref[:, 0, 0, :] = combine([(wide(c), x) for c, x in zip(sol, moved)])
    res_ref[:, 0, 0, :] = combine([(wide(c), x) for c, x in zip(res, moved)])
    for copy in sends:
        copy.wait_send()
    wait_all(plane_buf, plane_send, 0, PLANE - 1)
    wait_all(line_buf, line_send, 0, N_GZ - 1)


def local(right_side, elem_faces, elem_class, elem_scale, stretch, pml_flag, send_faces, blocks):
    vmem = pl.BlockSpec(memory_space=pltpu.VMEM)
    field = jax.ShapeDtypeStruct(right_side.shape, F32)
    given = (right_side, elem_faces, elem_class, elem_scale, stretch, pml_flag, send_faces, blocks)
    solution_field, residual = pl.pallas_call(
        kernel,
        out_shape=(field, field),
        in_specs=[pl.BlockSpec(memory_space=pltpu.HBM)] * len(given),
        out_specs=(vmem, vmem),
        scratch_shapes=[pltpu.VMEM(x.shape, x.dtype) for x in given]
        + [
            pltpu.VMEM((120, 640), F32),
            pltpu.VMEM((256, 1024), BF16),
            pltpu.VMEM((512, 896), BF16),
            pltpu.VMEM((896, 1024), BF16),
            pltpu.VMEM((1024, 512), F32),
            pltpu.VMEM((960, 512), BF16),
            pltpu.VMEM((320, 1024), BF16),
            pltpu.VMEM((960, LANES), F32),
            pltpu.VMEM((1024, 256), BF16),
            pltpu.VMEM((1024, 256), BF16),
            pltpu.VMEM((STEPS, 7, 40, LANES), F32),
            pltpu.VMEM((STEPS, 6, 40, LANES), F32),
            pltpu.VMEM((1, PLANE, 1, LANES), F32),
            pltpu.VMEM((1, N_GZ, 1, LANES), F32),
            pltpu.SemaphoreType.DMA((STEPS, 6)),
            pltpu.SemaphoreType.DMA((STEPS, 6)),
            pltpu.SemaphoreType.DMA((1,)),
            pltpu.SemaphoreType.DMA((1,)),
            pltpu.SemaphoreType.DMA((1,)),
            pltpu.SemaphoreType.DMA((1,)),
            pltpu.SemaphoreType.DMA((len(given),)),
        ],
        compiler_params=pltpu.CompilerParams(
            collective_id=0, has_side_effects=True, vmem_limit_bytes=56 * 1024 * 1024
        ),
    )(*given)
    return solution_field, residual


def solution(mesh):
    in_specs = (
        P(None, "gx", "gy", "gz"),
        P(None, "gx", "gy", "gz"),
        P("gx", "gy", "gz"),
        P("gx", "gy", "gz"),
        P(None, "gx", "gy", "gz"),
        P("gx", "gy", "gz"),
        P(None, "gx", "gy", "gz"),
        P(),
    )
    out_specs = (P(None, "gx", "gy", "gz"), P(None, "gx", "gy", "gz"))
    return jax.shard_map(local, mesh=mesh, in_specs=in_specs, out_specs=out_specs, check_vma=False)
```

time: 60.2 us -> 54.6 us (0.907)
  local copies, waits for them, and re-layouts: 5.1 us -> 2.2 us
  Pallas kernels: 53.4 us -> 51.5 us
  other arithmetic: 0.7 us -> 0 us
    pallas_call x1, Pallas kernels: 53.4 us -> 51.5 us  [local(): pl.pallas_call(kernel, out_shape=(field, field), in_specs=[pl.BlockSpec(m...]
    unnamed x13 -> x4, local copies, waits for them, and re-layouts: 3.78 us -> 2.2 us
    reshape x2 -> x0, local copies, waits for them, and re-layouts: 1.31 us -> none  [the longest x1 1.24 us: local(): blocks.reshape(120, 640)]
    unnamed x1 -> x0, other arithmetic: 0.7 us -> none
where the time goes in v2:
time: 54.6 us; the launch traced here: 54.4 us
  Pallas kernels  51.5 us (94%)
  local copies, waits for them, and re-layouts  2.2 us (4%)
  between operations  0.65 us (1%)
    pallas_call x1, Pallas kernels, local(): pl.pallas_call(kernel, out_shape=(field, field), in_specs=[pl.BlockSpec(m...  51.5 us
    unnamed x4, local copies, waits for them, and re-layouts  2.2 us

profile of v2, /device:TPU:1, one launch (start us, length us, event | category | flops | bytes accessed | tf_op | source)
XLA Modules:
  0.0 54.4 jit_solution(1599876698697601023)
XLA Ops:
  0.6 51.5 %shard_map.95 = (f32[40,1,1,512]{3,2,1,0:T(1,128)}, f32[40,1,1,512]{3,2,1,0:T(1,128)}) custom-call(f32[40,1,1,512]{3,2,1,0:T(1,128)} %rhs_in.1, s32[4,1,1,256]{3,2,1,0:T(1,128)} %faces_in.1, s32[1,1,256]{2,1,0:T(1,128)} %class_in.1, f32[1,1,256]{2,1,0:T(1,128)} %scale_in.1, f32[3,1,1,256]{3,2,1,0:T(1,128)} %stretch_in.1, s32[1,1,256]{2,1,0:T(1,128)} %flag_in.1, ...), custom_call_target="tpu_custom_call" | custom-call | tf_op jit(solution)/shard_map/pallas_call | solution.py:411
  52.2 0.0 copy-start
  52.2 1.6 %copy.12 = f32[40,1,1,512]{3,2,1,0:T(1,128)} copy(f32[40,1,1,512]{3,2,1,0:T(1,128)} %get-tuple-element.4) | data formatting | bytes 163840
  53.7 0.0 copy-done
  53.7 0.6 %copy.13 = f32[40,1,1,512]{3,2,1,0:T(1,128)} copy(f32[40,1,1,512]{3,2,1,0:T(1,128)S(1)} %copy-done) | data formatting | bytes 163840
Async XLA Ops:
  52.2 1.6 %copy-start = (f32[40,1,1,512]{3,2,1,0:T(1,128)S(1)}, f32[40,1,1,512]{3,2,1,0:T(1,128)}, u32[]{:S(2)}) copy-start(f32[40,1,1,512]{3,2,1,0:T(1,128)} %get-tuple-element.5) | copy-start | bytes 245764

commit v3 on v2

--- a/solution.py
+++ b/solution.py
@@ -59,8 +59,7 @@
     flag_in,
     send_in,
     blocks_in,
-    sol_ref,
-    res_ref,
+    out_ref,
     rhs_ref,
     faces_ref,
     class_ref,
@@ -73,6 +72,7 @@
     embed,
     place,
     pick,
+    pick_t,
     raw,
     smat,
     smat_t,
@@ -90,6 +90,8 @@
     line_send,
     line_recv,
     load_sem,
+    near_sem,
+    far_sem,
 ):
     at = {name: lax.axis_index(name) for name, _ in AXES}
     size = dict(AXES)
@@ -114,7 +116,7 @@
         line_devices.append(device(gz=lax.rem(at["gz"] + step, N_GZ)))
 
     barrier = pltpu.get_barrier_semaphore()
-    for other in plane_devices + line_devices:
+    for other in neighbours:
         pl.semaphore_signal(barrier, inc=1, device_id=other, device_id_type=MESH)
 
     loads = []
@@ -124,6 +126,13 @@
         copy = pltpu.make_async_copy(there, here, load_sem.at[i])
         copy.start()
         loads.append(copy)
+
+    def tell(sem, others):
+        for other in others:
+            pl.semaphore_signal(sem, inc=1, device_id=other, device_id_type=MESH)
+
+    def along(name, *steps):
+        return [device(**{name: lax.rem(at[name] + step, size[name])}) for step in steps]
 
     sends = []
 
@@ -176,10 +185,30 @@
         wait_all(line_buf, line_recv, which, N_GZ - 1)
         return jnp.sum(line_buf[which], axis=0)
 
+    face512 = lax.broadcasted_iota(jnp.int32, (512, LANES), 0)
+    no_face = jnp.full((1, 64), -1, jnp.int32)
+    loads[0].wait()
+    for k in range(6):
+        shared = jnp.concatenate([send_ref[k, 0], no_face], axis=1)
+        place[:, LANES * TILE[k] : LANES * (TILE[k] + 1)] = onehot(face512, shared)
+    loads[1].wait()
+    rhs = rhs_ref[:, 0, 0, :]
+    rhs_split = jnp.concatenate(pieces(rhs, 3), axis=0).astype(BF16)
+
+    def put(low, high):
+        placed = dot(rhs_split, place[:, LANES * low : LANES * high])
+        placed = placed[0:40] + placed[40:80] + placed[80:120]
+        for t in range(low, high):
+            part[0, t] = placed[:, LANES * (t - low) : LANES * (t - low + 1)]
+
+    put(5, 7)
+    put(0, 4)
+    pl.semaphore_wait(barrier, 6)
+    send_halo(0, (4, 5, 2, 3, 0, 1))
+
     position = lax.broadcasted_iota(jnp.int32, (1, 384), 1)
     target = ((position // 64) * 128 + jnp.where(position >= 256, 128, 0) + position % 64 + 1).astype(F32)
     face_col = lax.broadcasted_iota(jnp.int32, (512, 1), 0)
-    loads[0].wait()
     sent = jnp.concatenate([send_ref[k, 0] for k in range(6)], axis=1)
     found = jnp.sum(jnp.where(face_col == sent, target, 0.0), axis=1, keepdims=True)
     inner = jnp.broadcast_to(jnp.where(found > 0.0, 0.0, 1.0), (512, LANES)).astype(BF16)
@@ -188,25 +217,16 @@
     ).astype(BF16)
     rank = dot(below, inner)
     new_place = jnp.where(jnp.broadcast_to(found, (512, LANES)) > 0.0, found - 1.0, 512.0 + rank)
-    new_int = new_place.astype(jnp.int32)
     lane512 = lax.broadcasted_iota(jnp.int32, (512, LANES), 1)
-    for t in range(7):
-        place[:, LANES * t : LANES * (t + 1)] = onehot(new_int, lane512 + LANES * t)
-
-    loads[1].wait()
-    rhs = rhs_ref[:, 0, 0, :]
-    placed = dot(jnp.concatenate(pieces(rhs, 3), axis=0).astype(BF16), place[...])
-    placed = placed[0:40] + placed[40:80] + placed[80:120]
-    for t in range(7):
-        part[0, t] = placed[:, LANES * t : LANES * (t + 1)]
-    pl.semaphore_wait(barrier, len(plane_devices) + len(line_devices))
-    send_halo(0, (4, 5, 2, 3, 0, 1))
+    place[:, 512:640] = onehot(new_place.astype(jnp.int32), lane512 + 512)
+    put(4, 5)
 
     place_row = new_place.T[0:8, :]
     high = jnp.floor(place_row * (1.0 / 32.0))
     digits = jnp.concatenate([high, place_row - 32.0 * high], axis=0).astype(BF16)
     row512 = lax.broadcasted_iota(jnp.int32, (512, 256), 0)
     row128 = lax.broadcasted_iota(jnp.int32, (LANES, 256), 0)
+    lane256 = lax.broadcasted_iota(jnp.int32, (256, LANES), 1)
     loads[2].wait()
     for f in range(4):
         old = faces_ref[f, 0]
@@ -216,6 +236,9 @@
         new = jnp.where(old < 512, owned, (slot // 64) * 128 + jnp.where(slot >= 256, 128, 0) + 64 + slot % 64)
         for t in range(7):
             pick[LANES * t : LANES * (t + 1), 256 * f : 256 * (f + 1)] = onehot(row128 + LANES * t, new)
+        column = jnp.broadcast_to(new.astype(F32), (LANES, 256)).T.astype(jnp.int32)
+        for t in range(7):
+            pick_t[256 * f : 256 * (f + 1), LANES * t : LANES * (t + 1)] = onehot(column, lane256 + LANES * t)
 
     embed[...] = onehot(lax.broadcasted_iota(jnp.int32, (256, 1024), 0), embed_rows())
     loads[3].wait()
@@ -271,7 +294,7 @@
         split = jnp.concatenate(pieces(wide, 3), axis=0).astype(BF16)
         for tiles, directions in (((5, 6), (4, 5)), ((2, 3), (2, 3)), ((0, 1), (0, 1)), ((4,), ())):
             low = LANES * tiles[0]
-            spread = dot_nt(split, pick[low : low + LANES * len(tiles), :])
+            spread = dot(split, pick_t[:, low : low + LANES * len(tiles)])
             spread = spread[0:40] + spread[40:80] + spread[80:120]
             for n, t in enumerate(tiles):
                 part[step, t] = spread[:, LANES * n : LANES * (n + 1)]
@@ -337,22 +360,29 @@
         basis.append(early + late)
         return picked
 
-    def inner(i, j):
+    def add_inner(i, j):
         sums[i, j] = product(masked[i], basis[j])
 
     for step in range(3):
-        project(advance(step), False)
+        if step == 1:
+            pl.semaphore_wait(near_sem, 4)
+            tell(far_sem, along("gz", 4, 12) + along("gy", 1, 2, 3))
+        picked = advance(step)
+        if step == 0:
+            tell(near_sem, along("gz", 2, 14) + along("gx", 2, 6))
+        project(picked, False)
         masked.append(own(basis[step]))
         scatter(step + 1)
         for i in range(step + 1):
-            inner(i, step)
+            add_inner(i, step)
         if step:
             moved += back([basis[step]])
     energy = project(advance(3), True)
     masked.append(own(basis[3]))
     for i in range(4):
-        inner(i, 3)
+        add_inner(i, 3)
     pairs = [(i, j) for i in range(4) for j in range(i, 4)]
+    pl.semaphore_wait(far_sem, 5)
     start_plane(0, to_lanes([sums[pair] for pair in pairs] + [sums[3, 3] + energy_row(energy)]))
     scatter(4)
     plane_to_line(0)
@@ -396,8 +426,8 @@
     def wide(line):
         return jnp.concatenate([line] * 4, axis=1)
 
-    sol_ref[:, 0, 0, :] = combine([(wide(c), x) for c, x in zip(sol, moved)])
-    res_ref[:, 0, 0, :] = combine([(wide(c), x) for c, x in zip(res, moved)])
+    out_ref[0, :, 0, 0, :] = combine([(wide(c), x) for c, x in zip(sol, moved)])
+    out_ref[1, :, 0, 0, :] = combine([(wide(c), x) for c, x in zip(res, moved)])
     for copy in sends:
         copy.wait_send()
     wait_all(plane_buf, plane_send, 0, PLANE - 1)
@@ -406,19 +436,20 @@
 
 def local(right_side, elem_faces, elem_class, elem_scale, stretch, pml_flag, send_faces, blocks):
     vmem = pl.BlockSpec(memory_space=pltpu.VMEM)
-    field = jax.ShapeDtypeStruct(right_side.shape, F32)
+    fields = jax.ShapeDtypeStruct((2, *right_side.shape), F32)
     given = (right_side, elem_faces, elem_class, elem_scale, stretch, pml_flag, send_faces, blocks)
-    solution_field, residual = pl.pallas_call(
+    both = pl.pallas_call(
         kernel,
-        out_shape=(field, field),
-        in_specs=[pl.BlockSpec(memory_space=pltpu.HBM)] * len(given),
-        out_specs=(vmem, vmem),
+        out_shape=fields,
+        in_specs=[pl.BlockSpec(memory_space=pl.ANY)] * len(given),
+        out_specs=vmem,
         scratch_shapes=[pltpu.VMEM(x.shape, x.dtype) for x in given]
         + [
             pltpu.VMEM((120, 640), F32),
             pltpu.VMEM((256, 1024), BF16),
             pltpu.VMEM((512, 896), BF16),
             pltpu.VMEM((896, 1024), BF16),
+            pltpu.VMEM((1024, 896), BF16),
             pltpu.VMEM((1024, 512), F32),
             pltpu.VMEM((960, 512), BF16),
             pltpu.VMEM((320, 1024), BF16),
@@ -436,12 +467,14 @@
             pltpu.SemaphoreType.DMA((1,)),
             pltpu.SemaphoreType.DMA((1,)),
             pltpu.SemaphoreType.DMA((len(given),)),
+            pltpu.SemaphoreType.REGULAR,
+            pltpu.SemaphoreType.REGULAR,
         ],
         compiler_params=pltpu.CompilerParams(
             collective_id=0, has_side_effects=True, vmem_limit_bytes=56 * 1024 * 1024
         ),
     )(*given)
-    return solution_field, residual
+    return both[0], both[1]
 
 
 def solution(mesh):

time: 54.6 us -> 50 us (0.916)
  Pallas kernels: 51.5 us -> 47.6 us
  local copies, waits for them, and re-layouts: 2.2 us -> 1.6 us
    pallas_call x1, Pallas kernels: 51.5 us -> 47.6 us  [local(): pl.pallas_call(kernel, out_shape=fields, in_specs=[pl.BlockSpec(memory_sp...]
    unnamed x4 -> x0, local copies, waits for them, and re-layouts: 2.2 us -> none
    squeeze x0 -> x1, local copies, waits for them, and re-layouts: none -> 1.6 us  [local(): return (both[0], both[1])]
where the time goes in v3:
time: 50 us; the launch traced here: 49.9 us
  Pallas kernels  47.6 us (95%)
  local copies, waits for them, and re-layouts  1.6 us (3%)
  between operations  0.64 us (1%)
    pallas_call x1, Pallas kernels, local(): pl.pallas_call(kernel, out_shape=fields, in_specs=[pl.BlockSpec(memory_sp...  47.6 us
    squeeze x1, local copies, waits for them, and re-layouts, local(): return (both[0], both[1])  1.6 us

profile of v3, /device:TPU:1, one launch (start us, length us, event | category | flops | bytes accessed | tf_op | source)
XLA Modules:
  0.0 49.9 jit_solution(11737111419186530773)
XLA Ops:
  0.6 47.6 %shard_map.95 = f32[2,40,1,1,512]{4,3,2,1,0:T(1,128)} custom-call(f32[40,1,1,512]{3,2,1,0:T(1,128)} %rhs_in.1, s32[4,1,1,256]{3,2,1,0:T(1,128)} %faces_in.1, s32[1,1,256]{2,1,0:T(1,128)} %class_in.1, f32[1,1,256]{2,1,0:T(1,128)} %scale_in.1, f32[3,1,1,256]{3,2,1,0:T(1,128)} %stretch_in.1, s32[1,1,256]{2,1,0:T(1,128)} %flag_in.1, s32[6,1,1,64]{3,2,1,0:T(1,128)} %send_in.1, ...), custom_call_target="tpu_custom_call" | custom-call | tf_op jit(solution)/shard_map/pallas_call | solution.py:441
  48.3 1.6 %slice_bitcast_fusion = (f32[40,1,1,512]{3,2,1,0:T(1,128)}, f32[40,1,1,512]{3,2,1,0:T(1,128)}) fusion(f32[2,40,1,1,512]{4,3,2,1,0:T(1,128)} %shard_map.95), kind=kLoop, calls=%fused_computation | loop fusion | bytes 327680 | tf_op jit(solution)/shard_map/squeeze | solution.py:477

commit v4 on v3

--- a/solution.py
+++ b/solution.py
@@ -192,7 +192,7 @@
         shared = jnp.concatenate([send_ref[k, 0], no_face], axis=1)
         place[:, LANES * TILE[k] : LANES * (TILE[k] + 1)] = onehot(face512, shared)
     loads[1].wait()
-    rhs = rhs_ref[:, 0, 0, :]
+    rhs = jnp.concatenate([rhs_ref[pl.ds(c, 40, stride=4), :] for c in range(4)], axis=1)
     rhs_split = jnp.concatenate(pieces(rhs, 3), axis=0).astype(BF16)
 
     def put(low, high):
@@ -399,35 +399,33 @@
     gram[1, 4] = gram[2, 3]
     gram[0, 4] = gram[1, 3]
 
-    def apply(p):
-        out = [rho * p[0]]
-        for i in range(1, len(p)):
-            out.append(rho * p[i] + theta * p[i - 1])
-        return out + [theta * p[-1]]
-
-    def form(a, b):
-        return combine([(x, combine([(y, gram[i, j]) for j, y in enumerate(b)])) for i, x in enumerate(a)])
-
-    norm = gram[0, 0]
-    zero = jnp.zeros((1, LANES), F32)
-    sol, res, direction = [zero] * 4, [zero + 1.0], [zero + 1.0]
+    work = {(i, j): theta * gram[i, j + 1] + rho * gram[i, j] for i, j in pairs}
+    right = [gram[0, i] for i in range(4)]
+    factor, inverse = {}, []
     for i in range(4):
-        image = apply(direction)
-        alpha = norm / form(direction, image)
-        for j, x in enumerate(direction):
-            sol[j] = sol[j] + alpha * x
-        res = [x - alpha * y for x, y in zip(res + [zero], image)]
-        if i < 3:
-            new = form(res, res)
-            beta = new / norm
-            direction = [x + beta * y for x, y in zip(res, direction + [zero])]
-            norm = new
+        inverse.append(1.0 / work[i, i])
+        for j in range(i + 1, 4):
+            factor[i, j] = work[i, j] * inverse[i]
+        for j in range(i + 1, 4):
+            for k in range(j, 4):
+                work[j, k] = work[j, k] - factor[i, j] * work[i, k]
+            right[j] = right[j] - factor[i, j] * right[i]
+    sol = [right[i] * inverse[i] for i in range(4)]
+    for i in reversed(range(4)):
+        for j in range(i):
+            sol[j] = sol[j] - factor[j, i] * sol[i]
+    res = [1.0 - rho * sol[0]]
+    for i in range(1, 4):
+        res.append(-(rho * sol[i] + theta * sol[i - 1]))
+    res.append(-theta * sol[3])
 
     def wide(line):
         return jnp.concatenate([line] * 4, axis=1)
 
-    out_ref[0, :, 0, 0, :] = combine([(wide(c), x) for c, x in zip(sol, moved)])
-    out_ref[1, :, 0, 0, :] = combine([(wide(c), x) for c, x in zip(res, moved)])
+    for base, factors in ((0, sol), (160, res)):
+        value = combine([(wide(c), x) for c, x in zip(factors, moved)])
+        for c in range(4):
+            out_ref[pl.ds(base + c, 40, stride=4), :] = value[:, LANES * c : LANES * (c + 1)]
     for copy in sends:
         copy.wait_send()
     wait_all(plane_buf, plane_send, 0, PLANE - 1)
@@ -436,8 +434,8 @@
 
 def local(right_side, elem_faces, elem_class, elem_scale, stretch, pml_flag, send_faces, blocks):
     vmem = pl.BlockSpec(memory_space=pltpu.VMEM)
-    fields = jax.ShapeDtypeStruct((2, *right_side.shape), F32)
-    given = (right_side, elem_faces, elem_class, elem_scale, stretch, pml_flag, send_faces, blocks)
+    fields = jax.ShapeDtypeStruct((320, LANES), F32)
+    given = (right_side.reshape(160, LANES), elem_faces, elem_class, elem_scale, stretch, pml_flag, send_faces, blocks)
     both = pl.pallas_call(
         kernel,
         out_shape=fields,
@@ -471,10 +469,10 @@
             pltpu.SemaphoreType.REGULAR,
         ],
         compiler_params=pltpu.CompilerParams(
-            collective_id=0, has_side_effects=True, vmem_limit_bytes=56 * 1024 * 1024
+            collective_id=0, has_side_effects=True, vmem_limit_bytes=40 * 1024 * 1024
         ),
-    )(*given)
-    return both[0], both[1]
+    )(*[pltpu.with_memory_space_constraint(x, pltpu.HBM) for x in given])
+    return both[:160].reshape(right_side.shape), both[160:].reshape(right_side.shape)
 
 
 def solution(mesh):

time: 50 us -> 48.3 us (0.966)
  local copies, waits for them, and re-layouts: 1.6 us -> 0.67 us
  Pallas kernels: 47.6 us -> 46.9 us
    squeeze x1 -> x0, local copies, waits for them, and re-layouts: 1.6 us -> none  [local(): return (both[0], both[1])]
    pallas_call x1, Pallas kernels: 47.6 us -> 46.9 us  [local(): pl.pallas_call(kernel, out_shape=fields, in_specs=[pl.BlockSpec(memory_sp...]
    slice x0 -> x1, local copies, waits for them, and re-layouts: none -> 0.67 us  [local(): both[160:].reshape(right_side.shape)]
where the time goes in v4:
time: 48.3 us; the launch traced here: 48.2 us
  Pallas kernels  46.9 us (97%)
  local copies, waits for them, and re-layouts  0.67 us (1%)
  between operations  0.64 us (1%)
    pallas_call x1, Pallas kernels, local(): pl.pallas_call(kernel, out_shape=fields, in_specs=[pl.BlockSpec(memory_sp...  46.9 us

profile of v4, /device:TPU:1, one launch (start us, length us, event | category | flops | bytes accessed | tf_op | source)
XLA Modules:
  0.0 48.2 jit_solution(670408937575905279)
XLA Ops:
  0.6 46.9 %shard_map.95 = f32[320,128]{1,0:T(8,128)S(1)} custom-call(f32[160,128]{1,0:T(8,128)} %bitcast.3, s32[4,1,1,256]{3,2,1,0:T(1,128)} %faces_in.1, s32[1,1,256]{2,1,0:T(1,128)} %class_in.1, f32[1,1,256]{2,1,0:T(1,128)} %scale_in.1, f32[3,1,1,256]{3,2,1,0:T(1,128)} %stretch_in.1, s32[1,1,256]{2,1,0:T(1,128)} %flag_in.1, s32[6,1,1,64]{3,2,1,0:T(1,128)} %send_in.1, ...), custom_call_target="tpu_custom_call" | custom-call | tf_op jit(solution)/shard_map/pallas_call | solution.py:439
  47.5 0.7 %fusion = (f32[160,128]{1,0:T(8,128)}, f32[160,128]{1,0:T(8,128)}) fusion(f32[320,128]{1,0:T(8,128)S(1)} %shard_map.95), kind=kLoop, calls=%fused_computation | loop fusion | bytes 327680 | tf_op jit(solution)/shard_map/slice | solution.py:475

commit v5 on v4

--- a/solution.py
+++ b/solution.py
@@ -116,7 +116,7 @@
         line_devices.append(device(gz=lax.rem(at["gz"] + step, N_GZ)))
 
     barrier = pltpu.get_barrier_semaphore()
-    for other in neighbours:
+    for other in reversed(neighbours):
         pl.semaphore_signal(barrier, inc=1, device_id=other, device_id_type=MESH)
 
     loads = []
@@ -377,18 +377,25 @@
             add_inner(i, step)
         if step:
             moved += back([basis[step]])
-    energy = project(advance(3), True)
+    picked = advance(3)
+    pl.semaphore_wait(far_sem, 5)
     masked.append(own(basis[3]))
     for i in range(4):
         add_inner(i, 3)
     pairs = [(i, j) for i in range(4) for j in range(i, 4)]
-    pl.semaphore_wait(far_sem, 5)
-    start_plane(0, to_lanes([sums[pair] for pair in pairs] + [sums[3, 3] + energy_row(energy)]))
+    products = to_lanes([sums[pair] for pair in pairs] + [sums[3, 3]])
+    energy = jnp.sum(energy_row(project(picked, True)), axis=1, keepdims=True)
+    lane = lax.broadcasted_iota(jnp.int32, (1, LANES), 1)
+    start_plane(0, products + jnp.where(lane == len(pairs), energy, 0.0))
     scatter(4)
     plane_to_line(0)
     moved += back([basis[3]])
     advance(4)
     moved += back([basis[4]])
+    for copy in sends:
+        copy.wait_send()
+    wait_all(plane_buf, plane_send, 0, PLANE - 1)
+    wait_all(line_buf, line_send, 0, N_GZ - 1)
     totals = finish_line(0)
 
     gram = {}
@@ -426,10 +433,6 @@
         value = combine([(wide(c), x) for c, x in zip(factors, moved)])
         for c in range(4):
             out_ref[pl.ds(base + c, 40, stride=4), :] = value[:, LANES * c : LANES * (c + 1)]
-    for copy in sends:
-        copy.wait_send()
-    wait_all(plane_buf, plane_send, 0, PLANE - 1)
-    wait_all(line_buf, line_send, 0, N_GZ - 1)
 
 
 def local(right_side, elem_faces, elem_class, elem_scale, stretch, pml_flag, send_faces, blocks):

time: 48.3 us -> 48.1 us (level)
  no operation moved by 1% of the time
where the time goes in v5:
time: 48.1 us; the launch traced here: 48 us
  Pallas kernels  46.6 us (97%)
  local copies, waits for them, and re-layouts  0.67 us (1%)
  between operations  0.64 us (1%)
    pallas_call x1, Pallas kernels, local(): pl.pallas_call(kernel, out_shape=fields, in_specs=[pl.BlockSpec(memory_sp...  46.6 us

profile of v5, /device:TPU:1, one launch (start us, length us, event | category | flops | bytes accessed | tf_op | source)
XLA Modules:
  0.0 48.0 jit_solution(10465101692341493680)
XLA Ops:
  0.6 46.6 %shard_map.95 = f32[320,128]{1,0:T(8,128)S(1)} custom-call(f32[160,128]{1,0:T(8,128)} %bitcast.3, s32[4,1,1,256]{3,2,1,0:T(1,128)} %faces_in.1, s32[1,1,256]{2,1,0:T(1,128)} %class_in.1, f32[1,1,256]{2,1,0:T(1,128)} %scale_in.1, f32[3,1,1,256]{3,2,1,0:T(1,128)} %stretch_in.1, s32[1,1,256]{2,1,0:T(1,128)} %flag_in.1, s32[6,1,1,64]{3,2,1,0:T(1,128)} %send_in.1, ...), custom_call_target="tpu_custom_call" | custom-call | tf_op jit(solution)/shard_map/pallas_call | solution.py:442
  47.3 0.7 %fusion = (f32[160,128]{1,0:T(8,128)}, f32[160,128]{1,0:T(8,128)}) fusion(f32[320,128]{1,0:T(8,128)S(1)} %shard_map.95), kind=kLoop, calls=%fused_computation | loop fusion | bytes 327680 | tf_op jit(solution)/shard_map/slice | solution.py:478

commit v6 on v5

--- a/solution.py
+++ b/solution.py
@@ -15,7 +15,6 @@
 AXES = (("gx", N_GX), ("gy", N_GY), ("gz", N_GZ))
 PLANE = N_GX * N_GY
 LANES = 128
-EARLY = 640
 TILE = (0, 1, 2, 3, 5, 6)
 STEPS = 5
 
@@ -352,12 +351,15 @@
         def tile(t, got):
             return got if step == 0 else keep * basis[-1][t] + inv_theta * got
 
-        early = [tile(k, receive(step, k)) for k in range(4)] + [tile(4, part[step, 4])]
-        picked = gather(early, 0, EARLY) if step < 4 else None
-        late = [tile(TILE[k], receive(step, k)) for k in (4, 5)]
-        if step < 4:
-            picked = picked + gather(late, EARLY, 896)
-        basis.append(early + late)
+        tiles = {4: tile(4, part[step, 4])}
+        picked = gather([tiles[4]], 512, 640) if step < 4 else None
+        for pair in ((0, 1), (2, 3), (4, 5)):
+            for k in pair:
+                tiles[TILE[k]] = tile(TILE[k], receive(step, k))
+            if step < 4:
+                low, high = TILE[pair[0]], TILE[pair[1]]
+                picked = picked + gather([tiles[low], tiles[high]], LANES * low, LANES * (high + 1))
+        basis.append([tiles[t] for t in range(7)])
         return picked
 
     def add_inner(i, j):

time: 48.1 us -> 47.5 us (0.988)
  Pallas kernels: 46.6 us -> 46.1 us
    pallas_call x1, Pallas kernels: 46.6 us -> 46.1 us  [local(): pl.pallas_call(kernel, out_shape=fields, in_specs=[pl.BlockSpec(memory_sp...]
where the time goes in v6:
time: 47.5 us; the launch traced here: 47.4 us
  Pallas kernels  46.1 us (97%)
  local copies, waits for them, and re-layouts  0.67 us (1%)
  between operations  0.64 us (1%)
    pallas_call x1, Pallas kernels, local(): pl.pallas_call(kernel, out_shape=fields, in_specs=[pl.BlockSpec(memory_sp...  46.1 us

profile of v6, /device:TPU:1, one launch (start us, length us, event | category | flops | bytes accessed | tf_op | source)
XLA Modules:
  0.0 47.4 jit_solution(5831743959600555594)
XLA Ops:
  0.6 46.1 %shard_map.95 = f32[320,128]{1,0:T(8,128)S(1)} custom-call(f32[160,128]{1,0:T(8,128)} %bitcast.3, s32[4,1,1,256]{3,2,1,0:T(1,128)} %faces_in.1, s32[1,1,256]{2,1,0:T(1,128)} %class_in.1, f32[1,1,256]{2,1,0:T(1,128)} %scale_in.1, f32[3,1,1,256]{3,2,1,0:T(1,128)} %stretch_in.1, s32[1,1,256]{2,1,0:T(1,128)} %flag_in.1, s32[6,1,1,64]{3,2,1,0:T(1,128)} %send_in.1, ...), custom_call_target="tpu_custom_call" | custom-call | tf_op jit(solution)/shard_map/pallas_call | solution.py:444
  46.7 0.7 %fusion = (f32[160,128]{1,0:T(8,128)}, f32[160,128]{1,0:T(8,128)}) fusion(f32[320,128]{1,0:T(8,128)S(1)} %shard_map.95), kind=kLoop, calls=%fused_computation | loop fusion | bytes 327680 | tf_op jit(solution)/shard_map/slice | solution.py:480
